TPU v7x, 32 devices: a whole 2x2x4 slice. The times are simulated.
32 devices in a mesh: adapter: 8 (over z, y), tensor: 4 (over x, core).
Axes of the slice: x: 2, y: 2, z: 4, core: 2. Of those that a mesh axis runs over, the one named last changes fastest.
Arguments:
- partials: bfloat16 [4, 512, 8192], P('tensor', 'adapter'), may hold values from -4 to 4
- residual: bfloat16 [512, 8192], P('adapter'), may hold values from -80 to 80
- attention_norm_gain: bfloat16 [8192], replicated, may hold values from 0.25 to 1.75
- key_value_weight: bfloat16 [8192, 8, 256], P(None, 'tensor'), may hold values from -0.0625 to 0.0625
- adapter_down_weight: bfloat16 [8192, 8192], P('tensor', 'adapter'), may hold values from -0.0625 to 0.0625
- adapter_up_weight: bfloat16 [8192, 8, 256], P('adapter', 'tensor'), may hold values from -0.75 to 0.75
- row_adapter_index: int32 [512], P('adapter'), may hold values from 0 to 127, as said below
- queries: bfloat16 [512, 8192], P('adapter', 'tensor'), may hold values from -10 to 10
- key_value_cache: bfloat16 [64, 2, 1024, 1024], P('adapter', None, None, 'tensor'), may hold values from -10 to 10
- prompt_cache_length: int32 [64], P('adapter'), may hold values from 2 to 1024
Outputs:
- hidden_out: bfloat16 [512, 8192], P('adapter', 'tensor')
- new_kv: bfloat16 [512, 8, 256], P('adapter', 'tensor')
- attn_out: bfloat16 [512, 8192], P('adapter', 'tensor')
Inputs may be any that keep to these rules, and one draw needn't show every extreme that they name: `row_adapter_index`: adapter g is held by index g // 16 of the adapter axis. Of the 64 rows on one index of the adapter axis at most 32 use adapters held by one index; in every draw one index receives exactly 32 rows from every index.
All inputs are finite; a program needn't handle non-finite values.
Results may differ from a plain program's by a relative error of at most 0.012.
Values may be sent and summed in bfloat16 or wider, within the bound.
A program may use at most 128 MiB of HBM per device.

v0:
```python
import jax
import jax.numpy as jnp
from jax import lax
from jax.sharding import PartitionSpec as P

HEAD_SIZE = 128
ADAPTER_RANK = 64
FAN = 8


EPSILON = 1e-05
ADAPTER_SCALE = 0.5


def per_device(
    partials,
    residual,
    attention_norm_gain,
    key_value_weight,
    adapter_down_weight,
    adapter_up_weight,
    row_adapter_index,
    queries,
    key_value_cache,
    prompt_cache_length,
):
    row_dev = residual.shape[0]
    model_width = residual.shape[1]
    tensor_count = lax.axis_size("tensor")
    quarter = model_width // tensor_count
    tensor_index = lax.axis_index("tensor")
    flat_weight = key_value_weight.reshape(model_width, -1)
    partial_own = partials[0].astype(jnp.float32)
    summed = lax.psum(partial_own.astype(jnp.bfloat16), "tensor").astype(jnp.float32)
    hidden_full = (residual.astype(jnp.float32) + summed).astype(jnp.bfloat16)
    hidden_wide = hidden_full.astype(jnp.float32)
    mean_sq = jnp.mean(hidden_wide * hidden_wide, axis=1, keepdims=True)
    normed_full = (
        hidden_wide * lax.rsqrt(mean_sq + EPSILON) * attention_norm_gain.astype(jnp.float32)
    ).astype(jnp.bfloat16)
    hidden_part = lax.dynamic_slice_in_dim(hidden_full, tensor_index * quarter, quarter, 1)
    normed_part = lax.dynamic_slice_in_dim(normed_full, tensor_index * quarter, quarter, 1)
    base_kv = jnp.dot(normed_full, flat_weight, preferred_element_type=jnp.float32)
    adapt_count = lax.axis_size("adapter")
    capacity = max(2, 4 * row_dev // adapt_count)
    slot_count = adapt_count * capacity
    adapter_grouped = adapter_down_weight.shape[1] // ADAPTER_RANK
    owner_index = row_adapter_index // adapter_grouped
    local_id = row_adapter_index % adapter_grouped
    row_order = jnp.arange(row_dev)
    same_owner = owner_index[:, None] == owner_index[None, :]
    earlier = row_order[None, :] < row_order[:, None]
    slot_rank = jnp.sum((same_owner & earlier).astype(jnp.int32), axis=1)
    row_slot = owner_index * capacity + slot_rank
    row_to_slot = jnp.arange(slot_count)[:, None] == row_slot[None, :]
    slot_matrix = row_to_slot.astype(jnp.bfloat16)
    send_rows = (
        jnp.dot(slot_matrix, normed_part, preferred_element_type=jnp.float32)
        .astype(jnp.bfloat16)
        .reshape(adapt_count, capacity, quarter)
    )
    send_ids = (jnp.sum(jnp.where(row_to_slot, local_id[None, :] + 1, 0), axis=1) - 1).reshape(
        adapt_count, capacity
    )
    flattened_up = adapter_up_weight.reshape(adapter_grouped * ADAPTER_RANK, -1)
    rows_in = lax.all_to_all(send_rows, "adapter", split_axis=0, concat_axis=0, tiled=True)
    ids_in = lax.all_to_all(send_ids, "adapter", split_axis=0, concat_axis=0, tiled=True)
    item_count = rows_in.shape[1]
    flattened_rows = rows_in.reshape(-1, rows_in.shape[2])
    adapter_pick = ids_in.reshape(-1)[:, None] == jnp.arange(adapter_grouped)[None, :]
    projected_rows = jnp.dot(
        flattened_rows, adapter_down_weight, preferred_element_type=jnp.float32
    ).reshape(-1, adapter_grouped, ADAPTER_RANK)
    partial_low = jnp.sum(jnp.where(adapter_pick[:, :, None], projected_rows, 0.0), axis=1)
    reduced_rank_rows = lax.psum(partial_low.astype(jnp.bfloat16), "tensor")
    expanded_rows = jnp.where(
        adapter_pick[:, :, None], reduced_rank_rows[:, None, :], jnp.zeros((), jnp.bfloat16)
    ).reshape(-1, adapter_grouped * ADAPTER_RANK)
    adapter_update = (
        ADAPTER_SCALE * jnp.dot(expanded_rows, flattened_up, preferred_element_type=jnp.float32)
    ).astype(jnp.bfloat16)
    adapter_update = adapter_update.reshape(adapt_count, item_count, -1)
    returned = lax.all_to_all(adapter_update, "adapter", split_axis=0, concat_axis=0, tiled=True)
    returned = returned.reshape(slot_count, -1)
    update_rows = lax.dot_general(
        slot_matrix, returned, (((0,), (0,)), ((), ())), preferred_element_type=jnp.float32
    )
    local_heads = key_value_weight.shape[1]
    new_kv = (
        (base_kv + update_rows).astype(jnp.bfloat16).reshape(row_dev, local_heads, 2 * HEAD_SIZE)
    )
    local_prompts = key_value_cache.shape[0]
    cache_length = key_value_cache.shape[2]
    group_size = queries.shape[1] // (local_heads * HEAD_SIZE)
    score_scale = HEAD_SIZE ** (-0.5)
    query_heads = queries.reshape(local_prompts, FAN, local_heads, group_size, HEAD_SIZE)
    cache_keys = key_value_cache[:, 0].reshape(local_prompts, cache_length, local_heads, HEAD_SIZE)
    cache_values = key_value_cache[:, 1].reshape(
        local_prompts, cache_length, local_heads, HEAD_SIZE
    )
    scores = (
        jnp.einsum("pfkgd,pckd->pfkgc", query_heads, cache_keys, preferred_element_type=jnp.float32)
        * score_scale
    )
    valid_mask = jnp.arange(cache_length)[None, :] < prompt_cache_length[:, None]
    scores = jnp.where(valid_mask[:, None, None, None, :], scores, -jnp.inf)
    new_heads = new_kv.reshape(local_prompts, FAN, local_heads, 2 * HEAD_SIZE)
    own_key = new_heads[:, :, :, :HEAD_SIZE]
    own_value = new_heads[:, :, :, HEAD_SIZE:]
    own_score = (
        jnp.einsum("pfkgd,pfkd->pfkg", query_heads, own_key, preferred_element_type=jnp.float32)
        * score_scale
    )
    score_top = jnp.maximum(jnp.max(scores, axis=-1), own_score)
    weights = jnp.exp(scores - score_top[:, :, :, :, None]).astype(jnp.bfloat16)
    own_weight = jnp.exp(own_score - score_top).astype(jnp.bfloat16).astype(jnp.float32)
    weight_total = jnp.sum(weights, axis=-1, dtype=jnp.float32) + own_weight
    weighted = jnp.einsum(
        "pfkgc,pckd->pfkgd", weights, cache_values, preferred_element_type=jnp.float32
    )
    weighted = (
        weighted + own_weight[:, :, :, :, None] * own_value.astype(jnp.float32)[:, :, :, None, :]
    )
    attended = (weighted / weight_total[:, :, :, :, None]).astype(jnp.bfloat16).reshape(row_dev, -1)
    return (hidden_part, new_kv, attended)


def solution(mesh):
    return jax.shard_map(
        per_device,
        mesh=mesh,
        in_specs=(
            P("tensor", "adapter", None),
            P("adapter", None),
            P(),
            P(None, "tensor", None),
            P("tensor", "adapter"),
            P("adapter", "tensor", None),
            P("adapter"),
            P("adapter", "tensor"),
            P("adapter", None, None, "tensor"),
            P("adapter"),
        ),
        out_specs=(P("adapter", "tensor"), P("adapter", "tensor", None), P("adapter", "tensor")),
        check_vma=False,
    )
```

profile of v0, /device:TPU:0, one launch (start us, length us, event | category | flops | bytes accessed | tf_op | source)
XLA Modules:
  0.0 130.2 jit_solution(5828130885464203011)
XLA Ops:
  7.2 0.7 all-reduce.2.cloned.1.call-update
  7.9 0.7 and_select_fusion.1
  8.9 0.7 sub.25
  9.6 7.3 %all-to-all-start = ((s32[8,1,32]{2,1,0:T(1,128)}), s32[8,1,32]{2,1,0:T(1,128)S(1)}, u32[]{:S(2)}, u32[]{:S(2)}) async-start(s32[8,1,32]{2,1,0:T(1,128)} %sub.25), calls=%async_computation | async-start | bytes 8192 | tf_op jit(solution)/shard_map/all_to_all | solution.py:67
  16.8 0.7 convert_element_type.58
  17.6 8.2 %copy.40 = bf16[1024,8,2,256]{3,1,2,0:T(8,128)(2,1)} copy(bf16[1024,8,2,256]{3,2,1,0:T(2,128)(2,1)} %bitcast.72) | data formatting | bytes 16777216
  25.8 6.6 %copy.22 = bf16[2048,1024]{0,1:T(8,128)(2,1)} copy(bf16[2048,1024]{1,0:T(8,128)(2,1)} %param.14) | data formatting | bytes 8388608 | tf_op args[4]
  32.4 1.3 copy.41
  33.7 15.5 %all-reduce.2.cloned.1.call-done = bf16[64,8192]{1,0:T(8,128)(2,1)} async-done(((bf16[64,8192]{1,0:T(8,128)(2,1)}), bf16[64,8192]{1,0:T(8,128)(2,1)}) %all-reduce.2.cloned.1.call-update) | async-done | bytes 1048592 | tf_op jit(solution)/shard_map/psum | solution.py:34
  49.2 1.7 %fusion.2 = (f32[64]{0:T(128)S(1)}, bf16[64,8192]{1,0:T(8,128)(2,1)S(1)}) fusion(bf16[64,8192]{1,0:T(8,128)(2,1)} %all-reduce.2.cloned.1.call-done, bf16[64,8192]{1,0:T(8,128)(2,1)S(1)} %copy-done.3), kind=kLoop, calls=%fused_computation.9 | loop fusion | flops 3669952 | bytes 3145984 | tf_op jit(solution)/shard_map/reduce_sum | solution.py:37
  50.9 0.3 fusion.4
  51.3 1.5 %convolution_convert_fusion = bf16[256,2048]{1,0:T(8,128)(2,1)} fusion(bf16[64,8192]{1,0:T(8,128)(2,1)S(1)} %fusion.4, s32[]{:T(128)S(6)} %select_n.45, s32[64]{0:T(128)S(1)} %multiply_add_fusion), kind=kOutput, calls=%fused_computation.8 | convolution fusion | flops 67649536 | bytes 1311236 | tf_op jit(solution)/shard_map/dot_general | solution.py:58
  52.8 5.5 %all-to-all-start.1 = ((bf16[8,32,2048]{2,1,0:T(8,128)(2,1)}), bf16[8,32,2048]{2,1,0:T(8,128)(2,1)S(1)}, u32[]{:S(2)}, u32[]{:S(2)}) async-start(bf16[8,32,2048]{2,1,0:T(8,128)(2,1)} %bitcast.1), calls=%async_computation.1 | async-start | bytes 2097152 | tf_op jit(solution)/shard_map/all_to_all | solution.py:66
  58.3 5.7 %fusion.29 = (bf16[8,1,1024,256]{3,2,1,0:T(8,128)(2,1)}, bf16[8,1,1024,256]{3,2,1,0:T(8,128)(2,1)}) fusion(bf16[8,2,1024,256]{3,2,1,0:T(8,128)(2,1)} %param.18), kind=kLoop, calls=%fused_computation.59 | loop fusion | bytes 16777216 | tf_op jit(solution)/shard_map/slice | solution.py:97
  64.0 6.5 %copy.39 = bf16[8,1,1024,256]{2,3,0,1:T(8,128)(2,1)} copy(bf16[8,1,1024,256]{3,2,1,0:T(8,128)(2,1)} %get-tuple-element.8) | data formatting | bytes 8388608
  70.5 6.5 %copy.38 = bf16[8,1,1024,256]{2,3,0,1:T(8,128)(2,1)} copy(bf16[8,1,1024,256]{3,2,1,0:T(8,128)(2,1)} %get-tuple-element.7) | data formatting | bytes 8388608
  77.0 5.0 %bitcast_reduce_fusion = (f32[8,8,2,8]{3,1,2,0:T(8,128)S(1)}, f32[8,2,1024,8,8]{2,4,3,1,0:T(8,128)}) fusion(pred[8,1024]{1,0:T(8,128)(4,1)S(1)} %iota_compare_fusion.3, bf16[8,1024,2,128,1]{1,3,4,2,0:T(8,128)(2,1)} %bitcast.75, bf16[8,8,2,8,128]{4,1,3,2,0:T(8,128)(2,1)S(1)} %bitcast.69), kind=kOutput, calls=%fused_computation.1 | convolution fusion | flops 271580160 | bytes 8663040 | tf_op jit(solution)/shard_map/pfkgd,pckd->pfkgc/dot_general | solution.py:102
  82.1 0.5 broadcast.111
  82.6 0.7 reduce.3
  83.3 0.7 constant_dynamic-slice_fusion
  84.1 3.6 %fusion.5 = bf16[256,64]{0,1:T(8,128)(2,1)S(1)} fusion(bf16[256,2048,1]{1,0,2:T(8,128)(2,1)S(1)} %bitcast.79, bf16[16,64,2048]{2,1,0:T(8,128)(2,1)} %bitcast.74, pred[256,16]{0,1:T(8,128)(4,1)S(1)} %iota_compare_fusion.5), kind=kOutput, calls=%fused_computation.14 | convolution fusion | flops 1074249728 | bytes 5279744 | tf_op jit(solution)/shard_map/dot_general | solution.py:71
  87.6 10.3 %psum.15 = bf16[256,64]{0,1:T(8,128)(2,1)S(1)} all-reduce(bf16[256,64]{0,1:T(8,128)(2,1)S(1)} %fusion.5), channel_id=1, replica_groups=mesh['adapter'=8,'tensor'=4] {'tensor'}, use_global_device_ids=true, to_apply=%region_5.6 | all-reduce | flops 16384 | bytes 65536 | tf_op jit(solution)/shard_map/psum | solution.py:75
  98.0 1.2 fusion.8
  99.1 6.0 %all-to-all-start.2 = ((bf16[8,32,512]{2,1,0:T(8,128)(2,1)}), bf16[8,32,512]{2,1,0:T(8,128)(2,1)S(1)}, u32[]{:S(2)}, u32[]{:S(2)}) async-start(bf16[8,32,512]{2,1,0:T(8,128)(2,1)} %bitcast.7), calls=%async_computation.2 | async-start | bytes 524288 | tf_op jit(solution)/shard_map/all_to_all | solution.py:83
  105.1 4.9 %fusion.30 = f32[64,512]{1,0:T(8,128)S(1)} fusion(bf16[64,8192]{1,0:T(8,128)(2,1)S(1)} %fusion.4, bf16[8192,512]{1,0:T(8,128)(2,1)} %bitcast.71), kind=kOutput, calls=%fused_computation.60 | convolution fusion | flops 536870912 | bytes 9568256 | tf_op jit(solution)/shard_map/dot_general | solution.py:43
  110.1 3.9 %all-to-all-done.2 = bf16[8,32,512]{2,1,0:T(8,128)(2,1)S(1)} async-done(((bf16[8,32,512]{2,1,0:T(8,128)(2,1)}), bf16[8,32,512]{2,1,0:T(8,128)(2,1)S(1)}, u32[]{:S(2)}, u32[]{:S(2)}) %all-to-all-start.2) | async-done | bytes 262176 | tf_op jit(solution)/shard_map/all_to_all | solution.py:83
  113.9 0.2 fusion.10
  114.1 0.7 reshape.131
  114.8 0.3 fusion.14
  115.1 3.4 %convert_reduce_fusion = f32[8,8,2,8]{3,1,2,0:T(8,128)S(1)} fusion(f32[8,8,2,8]{3,1,2,0:T(8,128)S(1)} %fusion.17, f32[8,2,1024,8,8]{2,4,3,1,0:T(8,128)} %get-tuple-element.14, pred[8,1024]{1,0:T(8,128)(4,1)S(1)} %iota_compare_fusion.3), kind=kLoop, calls=%fused_computation.4 | loop fusion | flops 6290432 | bytes 4210688 | tf_op jit(solution)/shard_map/reduce_sum | solution.py:117
  118.5 4.0 %fusion.9 = bf16[8,8,2,8,128]{4,3,1,2,0:T(8,128)(2,1)S(1)} fusion(bf16[8,1024,2,128,1]{1,3,4,2,0:T(8,128)(2,1)S(1)} %bitcast.73, f32[8,8,2,8]{3,1,2,0:T(8,128)S(1)} %get-tuple-element.3, f32[8,8,2,128]{3,1,2,0:T(8,128)S(1)} %get-tuple-element.9, f32[8,8,2,8]{3,1,2,0:T(8,128)S(1)} %get-tuple-element.4, f32[8,2,1024,8,8]{2,4,3,1,0:T(8,128)} %get-tuple-element.14, ...), kind=kOutput, calls=%fused_computation.20 | convolution fusion | flops 273154048 | bytes 8736768 | tf_op jit(solution)/shard_map/pfkgc,pckd->pfkgd/dot_general | solution.py:118
  122.5 0.8 reshape.133
  (28 shorter events, 0.7 us)
Async XLA Ops:
  7.2 69.9 %copy-start = (bf16[64,2048]{1,0:T(8,128)(2,1)S(1)}, bf16[64,2048]{1,0:T(8,128)(2,1)}, u32[]{:S(2)}) copy-start(bf16[64,2048]{1,0:T(8,128)(2,1)} %param.17) | copy-start | bytes 786436
  7.2 42.0 %all-reduce.2.cloned.1.call-start = ((), (), s32[]{:S(2)}) async-start(), calls=%async_computation.3 | async-start | bytes 2097152 | tf_op jit(solution)/shard_map/psum | solution.py:34
  9.6 43.2 %all-to-all-start = ((s32[8,1,32]{2,1,0:T(1,128)}), s32[8,1,32]{2,1,0:T(1,128)S(1)}, u32[]{:S(2)}, u32[]{:S(2)}) async-start(s32[8,1,32]{2,1,0:T(1,128)} %sub.25), calls=%async_computation | async-start | bytes 8192 | tf_op jit(solution)/shard_map/all_to_all | solution.py:67
  25.8 6.6 %copy-start.2 = (bf16[1024,2,256]{2,1,0:T(2,128)(2,1)S(1)}, bf16[1024,2,256]{2,1,0:T(2,128)(2,1)}, u32[]{:S(2)}) copy-start(bf16[1024,2,256]{2,1,0:T(2,128)(2,1)} %param.15) | copy-start | bytes 3145732
  25.8 23.5 %copy-start.3 = (bf16[64,8192]{1,0:T(8,128)(2,1)S(1)}, bf16[64,8192]{1,0:T(8,128)(2,1)}, u32[]{:S(2)}) copy-start(bf16[64,8192]{1,0:T(8,128)(2,1)} %param.11) | copy-start | bytes 3145732
  52.8 31.3 %all-to-all-start.1 = ((bf16[8,32,2048]{2,1,0:T(8,128)(2,1)}), bf16[8,32,2048]{2,1,0:T(8,128)(2,1)S(1)}, u32[]{:S(2)}, u32[]{:S(2)}) async-start(bf16[8,32,2048]{2,1,0:T(8,128)(2,1)} %bitcast.1), calls=%async_computation.1 | async-start | bytes 2097152 | tf_op jit(solution)/shard_map/all_to_all | solution.py:66
  70.5 6.5 %copy-start.5 = (s32[8]{0:T(128)S(1)}, s32[8]{0:T(128)}, u32[]{:S(2)}) copy-start(s32[8]{0:T(128)} %param.19) | copy-start | bytes 100
  84.1 13.9 %copy-start.4 = (bf16[128,8,2,256]{3,1,2,0:T(8,128)(2,1)S(1)}, bf16[128,8,2,256]{3,1,2,0:T(8,128)(2,1)}, u32[]{:S(2)}) copy-start(bf16[128,8,2,256]{3,1,2,0:T(8,128)(2,1)} %copy.41) | copy-start | bytes 3145732
  99.1 14.8 %all-to-all-start.2 = ((bf16[8,32,512]{2,1,0:T(8,128)(2,1)}), bf16[8,32,512]{2,1,0:T(8,128)(2,1)S(1)}, u32[]{:S(2)}, u32[]{:S(2)}) async-start(bf16[8,32,512]{2,1,0:T(8,128)(2,1)} %bitcast.7), calls=%async_computation.2 | async-start | bytes 524288 | tf_op jit(solution)/shard_map/all_to_all | solution.py:83
  114.8 3.7 %copy-start.1 = (bf16[8,1,1024,256]{2,3,0,1:T(8,128)(2,1)S(1)}, bf16[8,1,1024,256]{2,3,0,1:T(8,128)(2,1)}, u32[]{:S(2)}) copy-start(bf16[8,1,1024,256]{2,3,0,1:T(8,128)(2,1)} %copy.39) | copy-start | bytes 12582916
Sparse Core Ops, SparseCore 0:
  10.4 38.8 all-reduce.1
where the time goes:
time: 131 us; the launch traced here: 130 us
  local copies, waits for them, and re-layouts  38.3 us (29%)
  matrix products  20.7 us (16%)
  waiting for transfers between devices  20.1 us (15%)
  starting transfers between devices  18.8 us (14%)
  between operations  14.2 us (11%)
  blocking collectives  10.3 us (8%)
  other arithmetic  7.9 us (6%)
    unnamed x17, local copies, waits for them, and re-layouts  29.1 us
    psum x1, waiting for transfers between devices, per_device(): lax.psum(partial_own.astype(jnp.bfloat16), 'tensor').astype(jnp.float32)  15.5 us
    psum x1, blocking collectives, per_device(): reduced_rank_rows = lax.psum(partial_low.astype(jnp.bfloat16), 'tensor')  10.3 us
    all_to_all x1, starting transfers between devices, per_device(): lax.all_to_all(send_ids, 'adapter', split_axis=0, concat_axis=0, tiled=True)  7.28 us
    all_to_all x1, starting transfers between devices, per_device(): lax.all_to_all(adapter_update, 'adapter', split_axis=0, concat_axis=0, ti...  6 us
    slice x1, local copies, waits for them, and re-layouts, per_device(): key_value_cache[:, 0]  5.72 us
    all_to_all x1, starting transfers between devices, per_device(): lax.all_to_all(send_rows, 'adapter', split_axis=0, concat_axis=0, tiled=T...  5.52 us
    dot_general x1, matrix products, per_device(): jnp.einsum('pfkgd,pckd->pfkgc', query_heads, cache_keys, preferred_elemen...  5.04 us
  transfers between devices with their start and end apart: 4, of which 2 were waited for; matrix products, arithmetic and copies ran while one was open for 40% of the time, Pallas kernels for 0%

commit v1 on v0

v1 whole, which is shorter than its diff:
```python
import functools

import jax
import jax.numpy as jnp
from jax import lax
from jax.experimental import pallas as pl
from jax.experimental.pallas import tpu as pltpu
from jax.sharding import PartitionSpec as P

HEAD_SIZE = 128
ADAPTER_RANK = 64
FAN = 8
EPSILON = 1e-05
ADAPTER_SCALE = 0.5
MESH = pl.DeviceIdType.MESH
F32 = jnp.float32
BF16 = jnp.bfloat16
SCALE = HEAD_SIZE ** (-0.5)


def cache_kernel(lengths, q_ref, kv_ref, acc_ref, top_ref, total_ref):
    length = lengths[pl.program_id(0)]
    kv_heads = kv_ref.shape[3] // HEAD_SIZE
    group = q_ref.shape[1] // HEAD_SIZE // kv_heads
    q = q_ref[...].astype(F32)
    lane = lax.broadcasted_iota(jnp.int32, (FAN, 128), 1)
    tops = jnp.zeros((FAN, 128), F32)
    totals = jnp.zeros((FAN, 128), F32)
    for k in range(kv_heads):
        cols = slice(k * HEAD_SIZE, (k + 1) * HEAD_SIZE)
        stack = jnp.concatenate(
            [q[:, (k * group + g) * HEAD_SIZE:(k * group + g + 1) * HEAD_SIZE] for g in range(group)], axis=0
        ).astype(BF16)
        scores = lax.dot_general(
            stack, kv_ref[0, 0, :, cols], (((1,), (1,)), ((), ())), preferred_element_type=F32
        ) * SCALE
        slot = lax.broadcasted_iota(jnp.int32, scores.shape, 1)
        scores = jnp.where(slot < length, scores, -jnp.inf)
        top = jnp.max(scores, axis=1, keepdims=True)
        weights = jnp.exp(scores - top).astype(BF16)
        total = jnp.sum(weights.astype(F32), axis=1, keepdims=True)
        acc = jnp.dot(weights, kv_ref[0, 1, :, cols], preferred_element_type=F32)
        for g in range(group):
            h = k * group + g
            rows = slice(g * FAN, (g + 1) * FAN)
            acc_ref[:, h * HEAD_SIZE:(h + 1) * HEAD_SIZE] = acc[rows]
            tops = jnp.where(lane == h, top[rows], tops)
            totals = jnp.where(lane == h, total[rows], totals)
    top_ref[...] = tops
    total_ref[...] = totals


def attend_cache(queries, cache, lengths):
    prompts, _, slots, width = cache.shape
    rows, q_width = queries.shape
    return pl.pallas_call(
        cache_kernel,
        out_shape=(
            jax.ShapeDtypeStruct((rows, q_width), F32),
            jax.ShapeDtypeStruct((rows, 128), F32),
            jax.ShapeDtypeStruct((rows, 128), F32),
        ),
        grid_spec=pltpu.PrefetchScalarGridSpec(
            num_scalar_prefetch=1,
            grid=(prompts,),
            in_specs=[
                pl.BlockSpec((FAN, q_width), lambda p, n: (p, 0)),
                pl.BlockSpec((1, 2, slots, width), lambda p, n: (p, 0, 0, 0)),
            ],
            out_specs=(
                pl.BlockSpec((FAN, q_width), lambda p, n: (p, 0)),
                pl.BlockSpec((FAN, 128), lambda p, n: (p, 0)),
                pl.BlockSpec((FAN, 128), lambda p, n: (p, 0)),
            ),
        ),
        compiler_params=pltpu.CompilerParams(vmem_limit_bytes=16 * 2**20),
        cost_estimate=pl.CostEstimate(
            flops=4 * rows * q_width * slots, bytes_accessed=2 * cache.size + 4 * rows * q_width,
            transcendentals=rows * q_width // HEAD_SIZE * slots,
        ),
    )(lengths, queries, cache)


W_CHUNKS = 4


def rows_kernel(
    adapters, tensors, cap,
    hidden_ref, gain_ref, weight_hbm, down_hbm, up_ref, pick_ref, place_ref, ids_ref,
    q_ref, acc_ref, top_ref, total_ref,
    new_kv_ref, attn_ref,
    weight, down, normed, out_rows, in_rows, low_out, low_in, delta, back, base,
    weight_sem, down_sem, row_send, row_recv, low_send, low_recv, back_send, back_recv,
):
    a = lax.axis_index("adapter")
    t = lax.axis_index("tensor")
    rows, width = hidden_ref.shape
    chunk = width // W_CHUNKS
    quarter = width // tensors
    slots = adapters * cap

    loads = [
        pltpu.make_async_copy(
            weight_hbm.at[pl.ds(i * chunk, chunk)], weight.at[pl.ds(i * chunk, chunk)], weight_sem.at[i]
        )
        for i in range(W_CHUNKS)
    ]
    for load in loads:
        load.start()
    load_down = pltpu.make_async_copy(down_hbm, down, down_sem)
    load_down.start()

    barrier = pltpu.get_barrier_semaphore()

    def greet_adapter(d, carry):
        pl.semaphore_signal(barrier, inc=1, device_id=(lax.rem(a + d, adapters), t), device_id_type=MESH)
        return carry

    lax.fori_loop(1, adapters, greet_adapter, 0)
    for d in range(1, tensors):
        pl.semaphore_signal(barrier, inc=1, device_id=(a, lax.rem(t + d, tensors)), device_id_type=MESH)

    square = jnp.zeros((rows, 128), F32)
    for i in range(W_CHUNKS):
        part = hidden_ref[:, i * chunk:(i + 1) * chunk].astype(F32)
        part = part * part
        for j in range(chunk // 128):
            square = square + part[:, j * 128:(j + 1) * 128]
    inverse = lax.rsqrt(jnp.sum(square, axis=1, keepdims=True) / width + EPSILON)
    for i in range(W_CHUNKS):
        cols = slice(i * chunk, (i + 1) * chunk)
        normed[:, cols] = (
            hidden_ref[:, cols].astype(F32) * inverse * gain_ref[:, cols].astype(F32)
        ).astype(BF16)

    mine = normed[:, pl.ds(pl.multiple_of(t * quarter, quarter), quarter)]
    out_rows[...] = jnp.dot(pick_ref[...], mine, preferred_element_type=F32).astype(BF16).reshape(out_rows.shape)

    pl.semaphore_wait(barrier, adapters - 1 + tensors - 1)

    def row_copy(d):
        other = lax.rem(a + d, adapters)
        return pltpu.make_async_remote_copy(
            src_ref=out_rows.at[other], dst_ref=in_rows.at[a], send_sem=row_send.at[d],
            recv_sem=row_recv.at[adapters - d], device_id=(other, t), device_id_type=MESH,
        )

    def back_copy(d):
        other = lax.rem(a + d, adapters)
        return pltpu.make_async_remote_copy(
            src_ref=delta.at[other], dst_ref=back.at[a], send_sem=back_send.at[d],
            recv_sem=back_recv.at[adapters - d], device_id=(other, t), device_id_type=MESH,
        )

    def row_arrival(d):
        other = lax.rem(a + d, adapters)
        return pltpu.make_async_remote_copy(
            src_ref=out_rows.at[other], dst_ref=in_rows.at[other], send_sem=row_send.at[d],
            recv_sem=row_recv.at[d], device_id=(other, t), device_id_type=MESH,
        )

    def back_arrival(d):
        other = lax.rem(a + d, adapters)
        return pltpu.make_async_remote_copy(
            src_ref=delta.at[other], dst_ref=back.at[other], send_sem=back_send.at[d],
            recv_sem=back_recv.at[d], device_id=(other, t), device_id_type=MESH,
        )

    def each(function):
        def step(d, carry):
            function(d)
            return carry

        lax.fori_loop(1, adapters, step, 0)

    each(lambda d: row_copy(d).start())
    in_rows[a] = out_rows[a]

    for i in range(W_CHUNKS):
        loads[i].wait()
        part = jnp.dot(
            normed[:, i * chunk:(i + 1) * chunk], weight[i * chunk:(i + 1) * chunk, :], preferred_element_type=F32
        )
        base[...] = part if i == 0 else base[...] + part
    load_down.wait()

    each(lambda d: row_arrival(d).wait_recv())

    lane = lax.broadcasted_iota(jnp.int32, (slots, 128), 1)
    odd = jnp.where(lane >= ADAPTER_RANK, 1, 0)
    ids = ids_ref[...] - odd
    got = in_rows[...].reshape(slots, quarter)
    low = jnp.zeros((slots, 128), F32)
    wide = 2
    for j in range(0, down.shape[1] // 128, wide):
        part = jnp.dot(got, down[:, j * 128:(j + wide) * 128], preferred_element_type=F32)
        for i in range(wide):
            low = low + jnp.where(ids == 2 * (j + i), part[:, i * 128:(i + 1) * 128], 0.0)
    low_out[...] = low.astype(BF16)

    shares = []
    for d in range(1, tensors):
        other = lax.rem(t + d, tensors)
        share = pltpu.make_async_remote_copy(
            src_ref=low_out, dst_ref=low_in.at[tensors - d], send_sem=low_send.at[d],
            recv_sem=low_recv.at[tensors - d], device_id=(a, other), device_id_type=MESH,
        )
        share.start()
        shares.append(share)
    for share in shares:
        share.wait()
    for d in range(1, tensors):
        low = low + low_in[d].astype(F32)
    low = low.astype(BF16).astype(F32)

    spread = jnp.concatenate(
        [jnp.where(ids == 2 * j, low, 0.0).astype(BF16) for j in range(down.shape[1] // 128)], axis=1
    )
    delta[...] = (
        ADAPTER_SCALE * jnp.dot(spread, up_ref[...], preferred_element_type=F32)
    ).astype(BF16).reshape(delta.shape)
    each(lambda d: back_copy(d).start())
    back[a] = delta[a]
    each(lambda d: back_arrival(d).wait_recv())

    update = jnp.dot(place_ref[...], back[...].reshape(slots, -1), preferred_element_type=F32)
    new_kv = (base[...] + update).astype(BF16)
    new_kv_ref[...] = new_kv

    kv_heads = new_kv.shape[1] // (2 * HEAD_SIZE)
    group = q_ref.shape[1] // HEAD_SIZE // kv_heads
    for k in range(kv_heads):
        key = new_kv[:, 2 * k * HEAD_SIZE:(2 * k + 1) * HEAD_SIZE].astype(F32)
        value = new_kv[:, (2 * k + 1) * HEAD_SIZE:(2 * k + 2) * HEAD_SIZE].astype(F32)
        for g in range(group):
            h = k * group + g
            cols = slice(h * HEAD_SIZE, (h + 1) * HEAD_SIZE)
            own = jnp.sum(q_ref[:, cols].astype(F32) * key, axis=1, keepdims=True) * SCALE
            cache_top = top_ref[:, h:h + 1]
            top = jnp.maximum(cache_top, own)
            shrink = jnp.exp(cache_top - top)
            weight_own = jnp.exp(own - top).astype(BF16).astype(F32)
            attn_ref[:, cols] = (
                (acc_ref[:, cols] * shrink + weight_own * value)
                / (total_ref[:, h:h + 1] * shrink + weight_own)
            ).astype(BF16)

    each(lambda d: row_copy(d).wait_send())
    each(lambda d: back_copy(d).wait_send())


def finish_rows(
    adapters, tensors, cap, hidden, gain, weight, down, up, pick, place, ids, queries, acc, top, total
):
    rows, width = hidden.shape
    columns = weight.shape[1]
    slots = adapters * cap
    quarter = width // tensors
    vmem = pl.BlockSpec(memory_space=pltpu.VMEM)
    hbm = pl.BlockSpec(memory_space=pl.ANY)
    dma = pltpu.SemaphoreType.DMA
    return pl.pallas_call(
        functools.partial(rows_kernel, adapters, tensors, cap),
        out_shape=(
            jax.ShapeDtypeStruct((rows, columns), BF16),
            jax.ShapeDtypeStruct(queries.shape, BF16),
        ),
        in_specs=[vmem, vmem, hbm, hbm, vmem, vmem, vmem, vmem, vmem, vmem, vmem, vmem],
        out_specs=(vmem, vmem),
        scratch_shapes=[
            pltpu.VMEM(weight.shape, BF16),
            pltpu.VMEM(down.shape, BF16),
            pltpu.VMEM((rows, width), BF16),
            pltpu.VMEM((adapters, cap, quarter), BF16),
            pltpu.VMEM((adapters, cap, quarter), BF16),
            pltpu.VMEM((slots, 128), BF16),
            pltpu.VMEM((tensors, slots, 128), BF16),
            pltpu.VMEM((adapters, cap, columns), BF16),
            pltpu.VMEM((adapters, cap, columns), BF16),
            pltpu.VMEM((rows, columns), F32),
            dma((W_CHUNKS,)),
            dma,
            dma((adapters,)),
            dma((adapters,)),
            dma((tensors,)),
            dma((tensors,)),
            dma((adapters,)),
            dma((adapters,)),
        ],
        compiler_params=pltpu.CompilerParams(
            collective_id=0, has_side_effects=True, vmem_limit_bytes=40 * 2**20
        ),
        cost_estimate=pl.CostEstimate(
            flops=2 * rows * width * columns + 2 * slots * down.size, bytes_accessed=2 * (weight.size + down.size),
            transcendentals=0,
        ),
    )(hidden, gain, weight, down, up, pick, place, ids, queries, acc, top, total)


def per_device(
    partials,
    residual,
    attention_norm_gain,
    key_value_weight,
    adapter_down_weight,
    adapter_up_weight,
    row_adapter_index,
    queries,
    key_value_cache,
    prompt_cache_length,
):
    rows, width = residual.shape
    tensors = lax.axis_size("tensor")
    adapters = lax.axis_size("adapter")
    t = lax.axis_index("tensor")
    a = lax.axis_index("adapter")
    half = width // 2
    core = t % 2
    swap_core = [(i, i ^ 1) for i in range(tensors)]
    swap_chip = [(i, i ^ 2) for i in range(tensors)]

    cap = max(16, 4 * rows // adapters)
    held = adapter_down_weight.shape[1] // ADAPTER_RANK
    every = lax.all_gather(row_adapter_index, "adapter")
    owner = every // held
    order = jnp.arange(rows)
    earlier = (order[None, :] < order[:, None])[None]
    rank = jnp.sum(((owner[:, :, None] == owner[:, None, :]) & earlier).astype(jnp.int32), axis=2)
    slot_ids = jnp.arange(cap)
    here = (owner == a)[:, None, :] & (rank[:, None, :] == slot_ids[None, :, None])
    ids = jnp.sum(jnp.where(here, (every % held)[:, None, :] + 1, 0), axis=2).reshape(-1) - 1
    ids = jnp.broadcast_to(ids[:, None], (adapters * cap, 128))
    own_owner = row_adapter_index // held
    own_rank = jnp.sum(((own_owner[:, None] == own_owner[None, :]) & earlier[0]).astype(jnp.int32), axis=1)
    row_slot = own_owner * cap + own_rank
    slots = jnp.arange(adapters * cap)
    pick = (slots[:, None] == row_slot[None, :]).astype(BF16)
    place = (row_slot[:, None] == slots[None, :]).astype(BF16)

    give = lax.dynamic_slice_in_dim(partials[0], (1 - core) * half, half, 1)
    keep = lax.dynamic_slice_in_dim(partials[0], core * half, half, 1)
    taken = lax.ppermute(give, "tensor", swap_core)
    chip_sum = (keep.astype(F32) + taken.astype(F32)).astype(BF16)
    other_sum = lax.ppermute(chip_sum, "tensor", swap_chip)
    hidden_half = (
        lax.dynamic_slice_in_dim(residual, core * half, half, 1).astype(F32)
        + (chip_sum.astype(F32) + other_sum.astype(F32))
    ).astype(BF16)
    other_half = lax.ppermute(hidden_half, "tensor", swap_core)
    hidden = jnp.where(
        core == 0,
        jnp.concatenate([hidden_half, other_half], axis=1),
        jnp.concatenate([other_half, hidden_half], axis=1),
    )
    quarter = width // tensors
    hidden_part = lax.dynamic_slice_in_dim(hidden, t * quarter, quarter, 1)

    acc, top, total = attend_cache(queries, key_value_cache, prompt_cache_length)
    new_kv, attended = finish_rows(
        adapters, tensors, cap, hidden, attention_norm_gain[None, :],
        key_value_weight.reshape(width, -1), adapter_down_weight,
        adapter_up_weight.reshape(adapter_up_weight.shape[0], -1),
        pick, place, ids, queries, acc, top, total,
    )
    return hidden_part, new_kv.reshape(rows, key_value_weight.shape[1], 2 * HEAD_SIZE), attended


def solution(mesh):
    return jax.shard_map(
        per_device,
        mesh=mesh,
        in_specs=(
            P("tensor", "adapter", None),
            P("adapter", None),
            P(),
            P(None, "tensor", None),
            P("tensor", "adapter"),
            P("adapter", "tensor", None),
            P("adapter"),
            P("adapter", "tensor"),
            P("adapter", None, None, "tensor"),
            P("adapter"),
        ),
        out_specs=(P("adapter", "tensor"), P("adapter", "tensor", None), P("adapter", "tensor")),
        check_vma=False,
    )
```

time: 131 us -> 94.8 us (0.72)
  Pallas kernels: 0 us -> 47.4 us
  matrix products: 20.7 us -> 0 us
  local copies, waits for them, and re-layouts: 38.3 us -> 18 us
  starting transfers between devices: 18.8 us -> 2.15 us
  between operations: 14.2 us -> 1.48 us
  waiting for transfers between devices: 20.1 us -> 9.7 us
  other arithmetic: 7.9 us -> 3.12 us
  blocking collectives: 10.3 us -> 12.6 us
    pallas_call x0 -> x2, Pallas kernels: none -> 47.4 us  [the longest x1 40.4 us: finish_rows(): pl.pallas_call(functools.partial(rows_kernel, adapters, tensors, cap), ou...]
    dot_general x8 -> x0, matrix products: 20.7 us -> none  [the longest x1 5.04 us: per_device(): jnp.einsum('pfkgd,pckd->pfkgc', query_heads, cache_keys, preferred_elemen...]
    all_to_all x3 -> x0, starting transfers between devices: 18.8 us -> none  [the longest x1 7.28 us: per_device(): lax.all_to_all(send_ids, 'adapter', split_axis=0, concat_axis=0, tiled=True)]
    psum x1 -> x0, waiting for transfers between devices: 15.5 us -> none  [per_device(): lax.psum(partial_own.astype(jnp.bfloat16), 'tensor').astype(jnp.float32)]
    unnamed x17 -> x22, local copies, waits for them, and re-layouts: 29.1 us -> 15.2 us
    unnamed x0 -> x1, blocking collectives: none -> 12.6 us
    psum x1 -> x0, blocking collectives: 10.3 us -> none  [per_device(): reduced_rank_rows = lax.psum(partial_low.astype(jnp.bfloat16), 'tensor')]
    ppermute x0 -> x3, waiting for transfers between devices: none -> 9.7 us  [the longest x1 9.69 us: per_device(): other_sum = lax.ppermute(chip_sum, 'tensor', swap_chip)]
  transfers between devices with their start and end apart: 4 -> 3, of which waited for: 2 -> 1; matrix products, arithmetic and copies ran while one was open for 40% -> 13% of each run, Pallas kernels for 0% -> 7%
where the time goes in v1:
time: 94.8 us; the launch traced here: 94.5 us
  Pallas kernels  47.4 us (50%)
  local copies, waits for them, and re-layouts  18 us (19%)
  blocking collectives  12.6 us (13%)
  waiting for transfers between devices  9.7 us (10%)
  other arithmetic  3.12 us (3%)
  starting transfers between devices  2.15 us (2%)
  between operations  1.48 us (2%)
    pallas_call x1, Pallas kernels, finish_rows(): pl.pallas_call(functools.partial(rows_kernel, adapters, tensors, cap), ou...  40.4 us
    unnamed x22, local copies, waits for them, and re-layouts  15.2 us
    unnamed x1, blocking collectives  12.6 us
    ppermute x1, waiting for transfers between devices, per_device(): other_sum = lax.ppermute(chip_sum, 'tensor', swap_chip)  9.69 us
    pallas_call x1, Pallas kernels, attend_cache(): pl.pallas_call(cache_kernel, out_shape=(jax.ShapeDtypeStruct((rows, q_wid...  6.96 us
  transfers between devices with their start and end apart: 3, of which 1 were waited for; matrix products, arithmetic and copies ran while one was open for 13% of the time, Pallas kernels for 7%

profile of v1, /device:TPU:0, one launch (start us, length us, event | category | flops | bytes accessed | tf_op | source)
XLA Modules:
  0.0 94.5 jit_solution(14298737892910743459)
XLA Ops:
  0.7 1.2 %dynamic-slice_bitcast_fusion = bf16[64,4096]{1,0:T(8,128)(2,1)S(1)} fusion(bf16[1,64,8192]{2,1,0:T(8,128)(2,1)} %param.10, s32[]{:T(128)S(6)} %select_n.48), kind=kLoop, calls=%fused_computation.4 | loop fusion | bytes 1048580 | tf_op jit(solution)/shard_map/dynamic_slice | solution.py:340
  1.8 0.0 copy-start.7
  1.8 0.5 collective-permute-start
  2.4 0.7 and_select_fusion
  3.0 1.2 %dynamic-slice.2 = u32[1]{0:T(128)} dynamic-slice(u32[32]{0:T(128)} %constant.77, u32[]{:T(128)S(6)} %add.55), dynamic_slice_sizes={1} | dynamic-slice | bytes 12
  4.9 0.9 dynamic-update-slice
  5.8 12.6 %all-reduce = s32[512]{0:T(512)S(1)} all-reduce(s32[512]{0:T(512)S(1)} %dynamic-update-slice), channel_id=2, replica_groups=mesh['adapter'=8,'tensor'=4] {'adapter'}, use_global_device_ids=true, to_apply=%add | all-reduce | flops 512 | bytes 4096
  18.4 0.1 reshape.53
  18.5 0.2 convert_reduce_fusion.1
  18.7 0.3 convert_reduce_fusion
  19.0 0.0 collective-permute-done
  19.0 1.2 %fusion = bf16[64,4096]{1,0:T(8,128)(2,1)S(1)} fusion(bf16[64,4096]{1,0:T(8,128)(2,1)S(1)} %collective-permute-done, bf16[1,64,8192]{2,1,0:T(8,128)(2,1)} %param.10, s32[]{:T(128)S(6)} %select_n.47), kind=kLoop, calls=%fused_computation.2 | loop fusion | flops 1048576 | bytes 1572868 | tf_op jit(solution)/shard_map/convert_element_type | solution.py:343
  20.2 1.6 %collective-permute-start.1 = (bf16[64,4096]{1,0:T(8,128)(2,1)S(1)}, bf16[64,4096]{1,0:T(8,128)(2,1)S(1)}, u32[]{:S(2)}, u32[]{:S(2)}) collective-permute-start(bf16[64,4096]{1,0:T(8,128)(2,1)S(1)} %fusion), channel_id=1, source_target_pairs={{0,2},{1,3},{2,0},{3,1},{4,6},{5,7},{6,4},{7,5},{8,10},{9,11},{10,... | collective-permute-start | bytes 1572872 | tf_op jit(solution)/shard_map/ppermute | solution.py:344
  21.8 0.2 select_reduce_fusion
  22.0 9.7 %collective-permute-done.1 = bf16[64,4096]{1,0:T(8,128)(2,1)S(1)} collective-permute-done((bf16[64,4096]{1,0:T(8,128)(2,1)S(1)}, bf16[64,4096]{1,0:T(8,128)(2,1)S(1)}, u32[]{:S(2)}, u32[]{:S(2)}) %collective-permute-start.1) | collective-permute-done | bytes 524320 | tf_op jit(solution)/shard_map/ppermute | solution.py:344
  31.7 0.2 add_convert_fusion
  31.9 0.1 collective-permute-start.2
  32.0 0.1 sub.25
  32.1 8.1 %copy.13 = bf16[1024,8,2,256]{3,1,2,0:T(8,128)(2,1)} copy(bf16[1024,8,2,256]{3,2,1,0:T(2,128)(2,1)} %bitcast.12) | data formatting | bytes 16777216
  40.2 0.2 copy.14
  40.4 0.5 copy-done.6
  40.9 0.2 copy-done.2
  41.2 3.4 %copy-done = bf16[8,2,1024,256]{3,2,1,0:T(8,128)(2,1)S(1)} copy-done((bf16[8,2,1024,256]{3,2,1,0:T(8,128)(2,1)S(1)}, bf16[8,2,1024,256]{3,2,1,0:T(8,128)(2,1)}, u32[]{:S(2)}) %copy-start) | copy-done | bytes 8388632
  44.5 7.0 %shard_map.121 = (f32[64,2048]{1,0:T(8,128)S(1)}, f32[64,128]{1,0:T(8,128)S(1)}, f32[64,128]{1,0:T(8,128)S(1)}) custom-call(s32[8]{0:T(128)S(1)} %copy-done.3, bf16[64,2048]{1,0:T(8,128)(2,1)S(1)} %copy-done.2, bf16[8,2,1024,256]{3,2,1,0:T(8,128)(2,1)S(1)} %copy-done), custom_call_target="tpu_custom_call" | custom-call | flops 536870912 | bytes 8912896 | tf_op jit(solution)/shard_map/pallas_call | solution.py:56
  51.5 0.1 fusion.3.place_ref
  51.6 0.0 collective-permute-done.2
  51.6 0.2 maximum_select_fusion.hidden_ref
  51.9 0.1 broadcast_in_dim.19.ids_ref
  52.0 40.4 %shard_map.122 = (bf16[64,512]{1,0:T(8,128)(2,1)S(1)}, bf16[64,2048]{1,0:T(8,128)(2,1)S(1)}) custom-call(bf16[64,8192]{1,0:T(8,128)(2,1)S(1)} %maximum_select_fusion.hidden_ref, bf16[1,8192]{1,0:T(2,128)(2,1)S(1)} %broadcast_in_dim.12.gain_ref, bf16[8192,512]{1,0:T(8,128)(2,1)} %bitcast.11, bf16[2048,1024]{1,0:T(8,128)(2,1)S(1)} %copy-done.1, ...), custom_call_target="tpu_custom_call" | custom-call | flops 1610612736 | bytes 12582912 | tf_op jit(solution)/shard_map/pallas_call | solution.py:262
  92.4 0.6 reshape.51
  93.1 0.7 constant_dynamic-slice_fusion
  93.8 0.7 copy.17
  (20 shorter events, 0.1 us)
Async XLA Ops:
  0.6 31.1 %copy-start.5 = (bf16[64,8192]{1,0:T(8,128)(2,1)S(1)}, bf16[64,8192]{1,0:T(8,128)(2,1)}, u32[]{:S(2)}) copy-start(bf16[64,8192]{1,0:T(8,128)(2,1)} %param.11) | copy-start | bytes 3145732
  1.8 30.1 %copy-start.7 = (s32[64]{0:T(128)S(1)}, s32[64]{0:T(128)}, u32[]{:S(2)}) copy-start(s32[64]{0:T(128)} %param.16) | copy-start | bytes 772
  1.8 17.2 %collective-permute-start = (bf16[64,4096]{1,0:T(8,128)(2,1)S(1)}, bf16[64,4096]{1,0:T(8,128)(2,1)S(1)}, u32[]{:S(2)}, u32[]{:S(2)}) collective-permute-start(bf16[64,4096]{1,0:T(8,128)(2,1)S(1)} %dynamic-slice_bitcast_fusion), channel_id=1, source_target_pairs={{0,1},{1,0},{2,3},{3,2},{4,5},{5,4},{6,7},{7,6},{8,9},{9,8},{10,11... | collective-permute-start | bytes 1572872 | tf_op jit(solution)/shard_map/ppermute | solution.py:342
  20.2 11.5 %collective-permute-start.1 = (bf16[64,4096]{1,0:T(8,128)(2,1)S(1)}, bf16[64,4096]{1,0:T(8,128)(2,1)S(1)}, u32[]{:S(2)}, u32[]{:S(2)}) collective-permute-start(bf16[64,4096]{1,0:T(8,128)(2,1)S(1)} %fusion), channel_id=1, source_target_pairs={{0,2},{1,3},{2,0},{3,1},{4,6},{5,7},{6,4},{7,5},{8,10},{9,11},{10,... | collective-permute-start | bytes 1572872 | tf_op jit(solution)/shard_map/ppermute | solution.py:344
  31.9 19.7 %collective-permute-start.2 = (bf16[64,4096]{1,0:T(8,128)(2,1)S(1)}, bf16[64,4096]{1,0:T(8,128)(2,1)S(1)}, u32[]{:S(2)}, u32[]{:S(2)}) collective-permute-start(bf16[64,4096]{1,0:T(8,128)(2,1)S(1)} %add_convert_fusion), channel_id=1, source_target_pairs={{0,1},{1,0},{2,3},{3,2},{4,5},{5,4},{6,7},{7,6},{8,9},{9,8},{10,11... | collective-permute-start | bytes 1572872 | tf_op jit(solution)/shard_map/ppermute | solution.py:349
  32.1 8.1 %copy-start.4 = (bf16[1024,2,256]{2,1,0:T(2,128)(2,1)S(1)}, bf16[1024,2,256]{2,1,0:T(2,128)(2,1)}, u32[]{:S(2)}) copy-start(bf16[1024,2,256]{2,1,0:T(2,128)(2,1)} %param.15) | copy-start | bytes 3145732
  40.2 0.7 copy-start.6
  40.2 1.0 %copy-start.2 = (bf16[64,2048]{1,0:T(8,128)(2,1)S(1)}, bf16[64,2048]{1,0:T(8,128)(2,1)}, u32[]{:S(2)}) copy-start(bf16[64,2048]{1,0:T(8,128)(2,1)} %q_ref.3) | copy-start | bytes 786436
  40.2 1.0 %copy-start.3 = (s32[8]{0:T(128)S(1)}, s32[8]{0:T(128)}, u32[]{:S(2)}) copy-start(s32[8]{0:T(128)} %lengths.1) | copy-start | bytes 100
  41.2 3.4 %copy-start = (bf16[8,2,1024,256]{3,2,1,0:T(8,128)(2,1)S(1)}, bf16[8,2,1024,256]{3,2,1,0:T(8,128)(2,1)}, u32[]{:S(2)}) copy-start(bf16[8,2,1024,256]{3,2,1,0:T(8,128)(2,1)} %kv_ref.1) | copy-start | bytes 25165828
  44.5 7.4 %copy-start.1 = (bf16[2048,1024]{1,0:T(8,128)(2,1)S(1)}, bf16[2048,1024]{1,0:T(8,128)(2,1)}, u32[]{:S(2)}) copy-start(bf16[2048,1024]{1,0:T(8,128)(2,1)} %down_hbm.1) | copy-start | bytes 12582916

commit v2 on v1

--- a/solution.py
+++ b/solution.py
@@ -20,6 +20,17 @@
 
 def cache_kernel(lengths, q_ref, kv_ref, acc_ref, top_ref, total_ref):
     length = lengths[pl.program_id(0)]
+    slots = kv_ref.shape[2]
+    sizes = [slots // 4, slots // 2, slots]
+    for i, used in enumerate(sizes):
+        above = length > (sizes[i - 1] if i else 0)
+
+        @pl.when(above & (length <= used))
+        def attend():
+            attend_used(used, length, q_ref, kv_ref, acc_ref, top_ref, total_ref)
+
+
+def attend_used(used, length, q_ref, kv_ref, acc_ref, top_ref, total_ref):
     kv_heads = kv_ref.shape[3] // HEAD_SIZE
     group = q_ref.shape[1] // HEAD_SIZE // kv_heads
     q = q_ref[...].astype(F32)
@@ -32,14 +43,14 @@
             [q[:, (k * group + g) * HEAD_SIZE:(k * group + g + 1) * HEAD_SIZE] for g in range(group)], axis=0
         ).astype(BF16)
         scores = lax.dot_general(
-            stack, kv_ref[0, 0, :, cols], (((1,), (1,)), ((), ())), preferred_element_type=F32
+            stack, kv_ref[0, 0, :used, cols], (((1,), (1,)), ((), ())), preferred_element_type=F32
         ) * SCALE
         slot = lax.broadcasted_iota(jnp.int32, scores.shape, 1)
         scores = jnp.where(slot < length, scores, -jnp.inf)
         top = jnp.max(scores, axis=1, keepdims=True)
         weights = jnp.exp(scores - top).astype(BF16)
         total = jnp.sum(weights.astype(F32), axis=1, keepdims=True)
-        acc = jnp.dot(weights, kv_ref[0, 1, :, cols], preferred_element_type=F32)
+        acc = jnp.dot(weights, kv_ref[0, 1, :used, cols], preferred_element_type=F32)
         for g in range(group):
             h = k * group + g
             rows = slice(g * FAN, (g + 1) * FAN)
@@ -73,7 +84,7 @@
                 pl.BlockSpec((FAN, 128), lambda p, n: (p, 0)),
             ),
         ),
-        compiler_params=pltpu.CompilerParams(vmem_limit_bytes=16 * 2**20),
+        compiler_params=pltpu.CompilerParams(vmem_limit_bytes=58 * 2**20),
         cost_estimate=pl.CostEstimate(
             flops=4 * rows * q_width * slots, bytes_accessed=2 * cache.size + 4 * rows * q_width,
             transcendentals=rows * q_width // HEAD_SIZE * slots,
@@ -86,7 +97,7 @@
 
 def rows_kernel(
     adapters, tensors, cap,
-    hidden_ref, gain_ref, weight_hbm, down_hbm, up_ref, pick_ref, place_ref, ids_ref,
+    near_ref, far_ref, gain_ref, weight_hbm, down_hbm, up_ref, pick_ref, place_ref, ids_ref,
     q_ref, acc_ref, top_ref, total_ref,
     new_kv_ref, attn_ref,
     weight, down, normed, out_rows, in_rows, low_out, low_in, delta, back, base,
@@ -94,7 +105,7 @@
 ):
     a = lax.axis_index("adapter")
     t = lax.axis_index("tensor")
-    rows, width = hidden_ref.shape
+    rows, width = near_ref.shape[0], weight_hbm.shape[0]
     chunk = width // W_CHUNKS
     quarter = width // tensors
     slots = adapters * cap
@@ -120,21 +131,27 @@
     for d in range(1, tensors):
         pl.semaphore_signal(barrier, inc=1, device_id=(a, lax.rem(t + d, tensors)), device_id_type=MESH)
 
+    core = lax.rem(t, 2)
     square = jnp.zeros((rows, 128), F32)
-    for i in range(W_CHUNKS):
-        part = hidden_ref[:, i * chunk:(i + 1) * chunk].astype(F32)
-        part = part * part
-        for j in range(chunk // 128):
-            square = square + part[:, j * 128:(j + 1) * 128]
+    for half_ref in (near_ref, far_ref):
+        for i in range(2):
+            part = half_ref[:, i * quarter:(i + 1) * quarter].astype(F32)
+            part = part * part
+            for j in range(quarter // 128):
+                square = square + part[:, j * 128:(j + 1) * 128]
     inverse = lax.rsqrt(jnp.sum(square, axis=1, keepdims=True) / width + EPSILON)
-    for i in range(W_CHUNKS):
-        cols = slice(i * chunk, (i + 1) * chunk)
-        normed[:, cols] = (
-            hidden_ref[:, cols].astype(F32) * inverse * gain_ref[:, cols].astype(F32)
-        ).astype(BF16)
+    for half_ref, parity in ((near_ref, core), (far_ref, 1 - core)):
+        for i in range(2):
+            cols = pl.ds(pl.multiple_of((2 * i + parity) * quarter, quarter), quarter)
+            normed[:, cols] = (
+                half_ref[:, i * quarter:(i + 1) * quarter].astype(F32) * inverse * gain_ref[:, cols].astype(F32)
+            ).astype(BF16)
 
     mine = normed[:, pl.ds(pl.multiple_of(t * quarter, quarter), quarter)]
-    out_rows[...] = jnp.dot(pick_ref[...], mine, preferred_element_type=F32).astype(BF16).reshape(out_rows.shape)
+    out_rows[:, :, :quarter] = jnp.dot(
+        pick_ref[...], mine, preferred_element_type=F32
+    ).astype(BF16).reshape(adapters, cap, quarter)
+    out_rows[:, :, quarter:] = ids_ref[...].reshape(adapters, cap, 128)
 
     pl.semaphore_wait(barrier, adapters - 1 + tensors - 1)
 
@@ -187,15 +204,15 @@
     each(lambda d: row_arrival(d).wait_recv())
 
     lane = lax.broadcasted_iota(jnp.int32, (slots, 128), 1)
-    odd = jnp.where(lane >= ADAPTER_RANK, 1, 0)
-    ids = ids_ref[...] - odd
-    got = in_rows[...].reshape(slots, quarter)
+    odd = jnp.where(lane >= ADAPTER_RANK, 1.0, 0.0)
+    ids = in_rows[:, :, quarter:].reshape(slots, 128).astype(F32) - odd
+    got = in_rows[:, :, :quarter].reshape(slots, quarter)
     low = jnp.zeros((slots, 128), F32)
     wide = 2
     for j in range(0, down.shape[1] // 128, wide):
         part = jnp.dot(got, down[:, j * 128:(j + wide) * 128], preferred_element_type=F32)
         for i in range(wide):
-            low = low + jnp.where(ids == 2 * (j + i), part[:, i * 128:(i + 1) * 128], 0.0)
+            low = low + jnp.where(ids == 2.0 * (j + i), part[:, i * 128:(i + 1) * 128], 0.0)
     low_out[...] = low.astype(BF16)
 
     shares = []
@@ -214,7 +231,7 @@
     low = low.astype(BF16).astype(F32)
 
     spread = jnp.concatenate(
-        [jnp.where(ids == 2 * j, low, 0.0).astype(BF16) for j in range(down.shape[1] // 128)], axis=1
+        [jnp.where(ids == 2.0 * j, low, 0.0).astype(BF16) for j in range(down.shape[1] // 128)], axis=1
     )
     delta[...] = (
         ADAPTER_SCALE * jnp.dot(spread, up_ref[...], preferred_element_type=F32)
@@ -250,9 +267,9 @@
 
 
 def finish_rows(
-    adapters, tensors, cap, hidden, gain, weight, down, up, pick, place, ids, queries, acc, top, total
+    adapters, tensors, cap, near, far, gain, weight, down, up, pick, place, ids, queries, acc, top, total
 ):
-    rows, width = hidden.shape
+    rows, width = near.shape[0], weight.shape[0]
     columns = weight.shape[1]
     slots = adapters * cap
     quarter = width // tensors
@@ -265,14 +282,14 @@
             jax.ShapeDtypeStruct((rows, columns), BF16),
             jax.ShapeDtypeStruct(queries.shape, BF16),
         ),
-        in_specs=[vmem, vmem, hbm, hbm, vmem, vmem, vmem, vmem, vmem, vmem, vmem, vmem],
+        in_specs=[vmem, vmem, vmem, hbm, hbm, vmem, vmem, vmem, vmem, vmem, vmem, vmem, vmem],
         out_specs=(vmem, vmem),
         scratch_shapes=[
             pltpu.VMEM(weight.shape, BF16),
             pltpu.VMEM(down.shape, BF16),
             pltpu.VMEM((rows, width), BF16),
-            pltpu.VMEM((adapters, cap, quarter), BF16),
-            pltpu.VMEM((adapters, cap, quarter), BF16),
+            pltpu.VMEM((adapters, cap, quarter + 128), BF16),
+            pltpu.VMEM((adapters, cap, quarter + 128), BF16),
             pltpu.VMEM((slots, 128), BF16),
             pltpu.VMEM((tensors, slots, 128), BF16),
             pltpu.VMEM((adapters, cap, columns), BF16),
@@ -288,13 +305,13 @@
             dma((adapters,)),
         ],
         compiler_params=pltpu.CompilerParams(
-            collective_id=0, has_side_effects=True, vmem_limit_bytes=40 * 2**20
+            collective_id=0, has_side_effects=True, vmem_limit_bytes=59 * 2**20
         ),
         cost_estimate=pl.CostEstimate(
             flops=2 * rows * width * columns + 2 * slots * down.size, bytes_accessed=2 * (weight.size + down.size),
             transcendentals=0,
         ),
-    )(hidden, gain, weight, down, up, pick, place, ids, queries, acc, top, total)
+    )(near, far, gain, weight, down, up, pick, place, ids, queries, acc, top, total)
 
 
 def per_device(
@@ -313,54 +330,49 @@
     tensors = lax.axis_size("tensor")
     adapters = lax.axis_size("adapter")
     t = lax.axis_index("tensor")
-    a = lax.axis_index("adapter")
-    half = width // 2
     core = t % 2
     swap_core = [(i, i ^ 1) for i in range(tensors)]
     swap_chip = [(i, i ^ 2) for i in range(tensors)]
 
     cap = max(16, 4 * rows // adapters)
     held = adapter_down_weight.shape[1] // ADAPTER_RANK
-    every = lax.all_gather(row_adapter_index, "adapter")
-    owner = every // held
     order = jnp.arange(rows)
-    earlier = (order[None, :] < order[:, None])[None]
-    rank = jnp.sum(((owner[:, :, None] == owner[:, None, :]) & earlier).astype(jnp.int32), axis=2)
-    slot_ids = jnp.arange(cap)
-    here = (owner == a)[:, None, :] & (rank[:, None, :] == slot_ids[None, :, None])
-    ids = jnp.sum(jnp.where(here, (every % held)[:, None, :] + 1, 0), axis=2).reshape(-1) - 1
-    ids = jnp.broadcast_to(ids[:, None], (adapters * cap, 128))
+    earlier = order[None, :] < order[:, None]
     own_owner = row_adapter_index // held
-    own_rank = jnp.sum(((own_owner[:, None] == own_owner[None, :]) & earlier[0]).astype(jnp.int32), axis=1)
+    own_rank = jnp.sum(((own_owner[:, None] == own_owner[None, :]) & earlier).astype(jnp.int32), axis=1)
     row_slot = own_owner * cap + own_rank
     slots = jnp.arange(adapters * cap)
     pick = (slots[:, None] == row_slot[None, :]).astype(BF16)
+    local = (row_adapter_index % held)[None, :] + 1
+    ids = jnp.sum(jnp.where(slots[:, None] == row_slot[None, :], local, 0), axis=1) - 1
+    ids = jnp.broadcast_to(ids[:, None], (adapters * cap, 128)).astype(BF16)
     place = (row_slot[:, None] == slots[None, :]).astype(BF16)
 
-    give = lax.dynamic_slice_in_dim(partials[0], (1 - core) * half, half, 1)
-    keep = lax.dynamic_slice_in_dim(partials[0], core * half, half, 1)
-    taken = lax.ppermute(give, "tensor", swap_core)
-    chip_sum = (keep.astype(F32) + taken.astype(F32)).astype(BF16)
+    quarter = width // tensors
+
+    def quarters(array, parity):
+        return jnp.concatenate(
+            [lax.dynamic_slice_in_dim(array, (2 * i + parity) * quarter, quarter, 1) for i in range(2)], axis=1
+        )
+
+    taken = lax.ppermute(quarters(partials[0], 1 - core), "tensor", swap_core)
+    chip_sum = (quarters(partials[0], core).astype(F32) + taken.astype(F32)).astype(BF16)
     other_sum = lax.ppermute(chip_sum, "tensor", swap_chip)
-    hidden_half = (
-        lax.dynamic_slice_in_dim(residual, core * half, half, 1).astype(F32)
-        + (chip_sum.astype(F32) + other_sum.astype(F32))
+    flat_weight = key_value_weight.reshape(width, -1)
+    flat_up = adapter_up_weight.reshape(adapter_up_weight.shape[0], -1)
+    acc, top, total = attend_cache(queries, key_value_cache, prompt_cache_length)
+    other_sum, acc, top, total, flat_weight, flat_up, pick, place, ids = lax.optimization_barrier(
+        (other_sum, acc, top, total, flat_weight, flat_up, pick, place, ids)
+    )
+    near = (
+        quarters(residual, core).astype(F32) + (chip_sum.astype(F32) + other_sum.astype(F32))
     ).astype(BF16)
-    other_half = lax.ppermute(hidden_half, "tensor", swap_core)
-    hidden = jnp.where(
-        core == 0,
-        jnp.concatenate([hidden_half, other_half], axis=1),
-        jnp.concatenate([other_half, hidden_half], axis=1),
-    )
-    quarter = width // tensors
-    hidden_part = lax.dynamic_slice_in_dim(hidden, t * quarter, quarter, 1)
-
-    acc, top, total = attend_cache(queries, key_value_cache, prompt_cache_length)
+    far = lax.ppermute(near, "tensor", swap_core)
+    hidden_part = lax.dynamic_slice_in_dim(near, (t // 2) * quarter, quarter, 1)
+
     new_kv, attended = finish_rows(
-        adapters, tensors, cap, hidden, attention_norm_gain[None, :],
-        key_value_weight.reshape(width, -1), adapter_down_weight,
-        adapter_up_weight.reshape(adapter_up_weight.shape[0], -1),
-        pick, place, ids, queries, acc, top, total,
+        adapters, tensors, cap, near, far, attention_norm_gain[None, :],
+        flat_weight, adapter_down_weight, flat_up, pick, place, ids, queries, acc, top, total,
     )
     return hidden_part, new_kv.reshape(rows, key_value_weight.shape[1], 2 * HEAD_SIZE), attended
 

time: 94.8 us -> 78.9 us (0.83)
  blocking collectives: 12.6 us -> 0 us
  waiting for transfers between devices: 9.7 us -> 0.47 us
  Pallas kernels: 47.4 us -> 54.4 us
  starting transfers between devices: 2.15 us -> 3.39 us
  local copies, waits for them, and re-layouts: 18 us -> 16.9 us
    unnamed x1 -> x0, blocking collectives: 12.6 us -> none
    ppermute x1, waiting for transfers between devices: 9.69 us -> 0.01 us  [per_device(): other_sum = lax.ppermute(chip_sum, 'tensor', swap_chip)]
    pallas_call x1, Pallas kernels: 40.4 us -> 44.2 us  [finish_rows(): pl.pallas_call(functools.partial(rows_kernel, adapters, tensors, cap), ou...]
    unnamed x22 -> x13, local copies, waits for them, and re-layouts: 15.2 us -> 11.9 us
    pallas_call x1, Pallas kernels: 6.96 us -> 10.1 us  [attend_cache(): pl.pallas_call(cache_kernel, out_shape=(jax.ShapeDtypeStruct((rows, q_wid...]
    ppermute x1, starting transfers between devices: 1.56 us -> 2.8 us  [per_device(): other_sum = lax.ppermute(chip_sum, 'tensor', swap_chip)]
    convert_element_type x2 -> x3, other arithmetic: 1.36 us -> 0.32 us  [the longest x1 0.19 us: per_device(): near = (quarters(residual, core).astype(F32) + (chip_sum.astype(F32) + ot...]
    dynamic_slice x2 -> x3, local copies, waits for them, and re-layouts: 1.88 us -> 2.06 us  [the longest x2 1.34 us: quarters(): lax.dynamic_slice_in_dim(array, (2 * i + parity) * quarter, quarter, 1)]
  transfers between devices with their start and end apart: 3 -> 3, of which waited for: 1 -> 1; matrix products, arithmetic and copies ran while one was open for 13% -> 17% of each run, Pallas kernels for 7% -> 13%
where the time goes in v2:
time: 78.9 us; the launch traced here: 78.5 us
  Pallas kernels  54.4 us (69%)
  local copies, waits for them, and re-layouts  16.9 us (21%)
  starting transfers between devices  3.39 us (4%)
  other arithmetic  2.65 us (3%)
    pallas_call x1, Pallas kernels, finish_rows(): pl.pallas_call(functools.partial(rows_kernel, adapters, tensors, cap), ou...  44.2 us
    unnamed x13, local copies, waits for them, and re-layouts  11.9 us
    pallas_call x1, Pallas kernels, attend_cache(): pl.pallas_call(cache_kernel, out_shape=(jax.ShapeDtypeStruct((rows, q_wid...  10.1 us
    ppermute x1, starting transfers between devices, per_device(): other_sum = lax.ppermute(chip_sum, 'tensor', swap_chip)  2.8 us
  transfers between devices with their start and end apart: 3, of which 1 were waited for; matrix products, arithmetic and copies ran while one was open for 17% of the time, Pallas kernels for 13%

profile of v2, /device:TPU:0, one launch (start us, length us, event | category | flops | bytes accessed | tf_op | source)
XLA Modules:
  0.0 78.5 jit_solution(16043491526434398993)
XLA Ops:
  0.7 1.3 %dynamic-slice_bitcast_fusion.3 = (bf16[64,2048]{1,0:T(8,128)(2,1)S(1)}, bf16[64,2048]{1,0:T(8,128)(2,1)S(1)}, bf16[64,2048]{1,0:T(8,128)(2,1)S(1)}, bf16[64,2048]{1,0:T(8,128)(2,1)S(1)}) fusion(bf16[1,64,8192]{2,1,0:T(8,128)(2,1)} %param.10, s32[]{:T(128)S(6)} %select_n.44, s32[]{:T(128)S(6)} %select_n.45, s32[]{:T(128)S(6)} %select_n.47, s32[]{:T(128)S(6)} %select_n.46), kind=kLoop, calls=%fused_computation.6 | loop fusion | bytes 2097168 | tf_op jit(solution)/shard_map/dynamic_slice | solution.py:355
  2.0 0.5 collective-permute-start
  2.5 0.7 fusion.3
  3.2 0.2 convert_reduce_fusion
  3.4 0.1 select_reduce_fusion
  3.5 0.7 fusion.1.place_ref
  4.2 0.0 collective-permute-done
  4.2 0.1 add_convert_fusion.1
  4.3 2.8 %collective-permute-start.1 = (bf16[64,4096]{1,0:T(8,128)(2,1)S(1)}, bf16[64,4096]{1,0:T(8,128)(2,1)S(1)}, u32[]{:S(2)}, u32[]{:S(2)}) collective-permute-start(bf16[64,4096]{1,0:T(8,128)(2,1)S(1)} %add_convert_fusion.1), channel_id=1, source_target_pairs={{0,2},{1,3},{2,0},{3,1},{4,6},{5,7},{6,4},{7,5},{8,10},{9,11},{10,... | collective-permute-start | bytes 1572872 | tf_op jit(solution)/shard_map/ppermute | solution.py:360
  7.1 0.0 copy-start.1
  7.1 8.1 %copy.13 = bf16[1024,8,2,256]{3,1,2,0:T(8,128)(2,1)} copy(bf16[1024,8,2,256]{3,2,1,0:T(2,128)(2,1)} %bitcast.13) | data formatting | bytes 16777216
  15.3 0.0 copy-start.3
  15.3 0.0 copy-start.4
  15.3 0.0 copy-done.1
  15.3 1.3 %copy.14 = bf16[128,8,2,256]{3,1,2,0:T(8,128)(2,1)} copy(bf16[128,8,2,256]{3,2,1,0:T(2,128)(2,1)S(1)} %bitcast.15) | data formatting | bytes 2097152
  16.5 10.1 %shard_map.121 = (f32[64,2048]{1,0:T(8,128)}, f32[64,128]{1,0:T(8,128)}, f32[64,128]{1,0:T(8,128)}) custom-call(s32[8]{0:T(128)} %lengths.1, bf16[64,2048]{1,0:T(8,128)(2,1)} %q_ref.3, bf16[8,2,1024,256]{3,2,1,0:T(8,128)(2,1)} %kv_ref.1), custom_call_target="tpu_custom_call" | custom-call | flops 536870912 | bytes 8912896 | tf_op jit(solution)/shard_map/pallas_call | solution.py:67
  26.7 0.7 fusion.pick_ref
  27.3 0.0 copy-done.3
  27.4 0.0 collective-permute-done.1
  27.4 0.7 broadcast_in_dim.18.ids_ref
  28.1 0.2 add_convert_fusion.near_ref
  28.3 0.0 copy-start
  28.3 0.1 collective-permute-start.2
  28.4 0.0 copy-done.4
  28.4 0.7 broadcast_in_dim.19.gain_ref
  29.1 0.7 constant_dynamic-slice_fusion
  29.8 0.5 collective-permute-done.2.far_ref
  30.3 0.0 copy-done
  30.3 0.8 copy-done.2
  31.1 44.2 %shard_map.122 = (bf16[64,512]{1,0:T(8,128)(2,1)}, bf16[64,2048]{1,0:T(8,128)(2,1)}) custom-call(bf16[64,4096]{1,0:T(8,128)(2,1)} %copy-done, bf16[64,4096]{1,0:T(8,128)(2,1)} %copy-done.2, bf16[1,8192]{1,0:T(2,128)(2,1)} %broadcast_in_dim.19.gain_ref, bf16[8192,512]{1,0:T(8,128)(2,1)} %bitcast.12, bf16[2048,1024]{1,0:T(8,128)(2,1)} %down_hbm.1, ...), custom_call_target="tpu_custom_call" | custom-call | flops 1610612736 | bytes 12582912 | tf_op jit(solution)/shard_map/pallas_call | solution.py:279
  75.3 1.5 %reshape.30 = bf16[64,2,256]{2,1,0:T(2,128)(2,1)} reshape(bf16[64,512]{1,0:T(8,128)(2,1)} %get-tuple-element.29) | data formatting | bytes 131072 | tf_op jit(solution)/shard_map/reshape | solution.py:377
  76.8 1.7 %copy.16 = bf16[64,2048]{1,0:T(8,128)(2,1)} copy(bf16[64,2048]{1,0:T(8,128)(2,1)} %get-tuple-element.44) | data formatting | bytes 524288
  (5 shorter events, 0.1 us)
Async XLA Ops:
  2.0 2.2 %collective-permute-start = (bf16[64,4096]{1,0:T(8,128)(2,1)S(1)}, bf16[64,4096]{1,0:T(8,128)(2,1)S(1)}, u32[]{:S(2)}, u32[]{:S(2)}) collective-permute-start(bf16[64,4096]{1,0:T(8,128)(2,1)S(1)} %pad_maximum_fusion), channel_id=1, source_target_pairs={{0,1},{1,0},{2,3},{3,2},{4,5},{5,4},{6,7},{7,6},{8,9},{9,8},{10,11... | collective-permute-start | bytes 1572872 | tf_op jit(solution)/shard_map/ppermute | solution.py:358
  4.3 23.1 %collective-permute-start.1 = (bf16[64,4096]{1,0:T(8,128)(2,1)S(1)}, bf16[64,4096]{1,0:T(8,128)(2,1)S(1)}, u32[]{:S(2)}, u32[]{:S(2)}) collective-permute-start(bf16[64,4096]{1,0:T(8,128)(2,1)S(1)} %add_convert_fusion.1), channel_id=1, source_target_pairs={{0,2},{1,3},{2,0},{3,1},{4,6},{5,7},{6,4},{7,5},{8,10},{9,11},{10,... | collective-permute-start | bytes 1572872 | tf_op jit(solution)/shard_map/ppermute | solution.py:360
  7.1 8.1 %copy-start.1 = (bf16[1024,2,256]{2,1,0:T(2,128)(2,1)S(1)}, bf16[1024,2,256]{2,1,0:T(2,128)(2,1)}, u32[]{:S(2)}) copy-start(bf16[1024,2,256]{2,1,0:T(2,128)(2,1)} %param.15) | copy-start | bytes 3145732
  15.3 12.1 %copy-start.3 = (bf16[64,8192]{1,0:T(8,128)(2,1)S(1)}, bf16[64,8192]{1,0:T(8,128)(2,1)}, u32[]{:S(2)}) copy-start(bf16[64,8192]{1,0:T(8,128)(2,1)} %param.11) | copy-start | bytes 3145732
  15.3 13.2 %copy-start.4 = (bf16[8192]{0:T(1024)(128)(2,1)S(1)}, bf16[8192]{0:T(1024)(128)(2,1)}, u32[]{:S(2)}) copy-start(bf16[8192]{0:T(1024)(128)(2,1)} %param.12) | copy-start | bytes 49156
  28.3 2.0 %copy-start = (bf16[64,4096]{1,0:T(8,128)(2,1)}, bf16[64,4096]{1,0:T(8,128)(2,1)S(1)}, u32[]{:S(2)}) copy-start(bf16[64,4096]{1,0:T(8,128)(2,1)S(1)} %add_convert_fusion.near_ref) | copy-start | bytes 1572868
  28.3 2.0 %collective-permute-start.2 = (bf16[64,4096]{1,0:T(8,128)(2,1)S(1)}, bf16[64,4096]{1,0:T(8,128)(2,1)S(1)}, u32[]{:S(2)}, u32[]{:S(2)}) collective-permute-start(bf16[64,4096]{1,0:T(8,128)(2,1)S(1)} %add_convert_fusion.near_ref), channel_id=1, source_target_pairs={{0,1},{1,0},{2,3},{3,2},{4,5},{5,4},{6,7},{7,6},{8,9},{9,8},{10,11... | collective-permute-start | bytes 1572872 | tf_op jit(solution)/shard_map/ppermute | solution.py:370
  30.3 0.8 copy-start.2

commit v3 on v2

--- a/solution.py
+++ b/solution.py
@@ -18,78 +18,47 @@
 SCALE = HEAD_SIZE ** (-0.5)
 
 
-def cache_kernel(lengths, q_ref, kv_ref, acc_ref, top_ref, total_ref):
-    length = lengths[pl.program_id(0)]
-    slots = kv_ref.shape[2]
-    sizes = [slots // 4, slots // 2, slots]
-    for i, used in enumerate(sizes):
-        above = length > (sizes[i - 1] if i else 0)
-
-        @pl.when(above & (length <= used))
-        def attend():
-            attend_used(used, length, q_ref, kv_ref, acc_ref, top_ref, total_ref)
-
-
-def attend_used(used, length, q_ref, kv_ref, acc_ref, top_ref, total_ref):
-    kv_heads = kv_ref.shape[3] // HEAD_SIZE
+def attend_cache(q_ref, cache, length_ref, loads, acc_ref, top_ref, total_ref):
+    prompts, _, slots, width = cache.shape
+    kv_heads = width // HEAD_SIZE
     group = q_ref.shape[1] // HEAD_SIZE // kv_heads
-    q = q_ref[...].astype(F32)
     lane = lax.broadcasted_iota(jnp.int32, (FAN, 128), 1)
-    tops = jnp.zeros((FAN, 128), F32)
-    totals = jnp.zeros((FAN, 128), F32)
-    for k in range(kv_heads):
-        cols = slice(k * HEAD_SIZE, (k + 1) * HEAD_SIZE)
-        stack = jnp.concatenate(
-            [q[:, (k * group + g) * HEAD_SIZE:(k * group + g + 1) * HEAD_SIZE] for g in range(group)], axis=0
-        ).astype(BF16)
-        scores = lax.dot_general(
-            stack, kv_ref[0, 0, :used, cols], (((1,), (1,)), ((), ())), preferred_element_type=F32
-        ) * SCALE
-        slot = lax.broadcasted_iota(jnp.int32, scores.shape, 1)
-        scores = jnp.where(slot < length, scores, -jnp.inf)
-        top = jnp.max(scores, axis=1, keepdims=True)
-        weights = jnp.exp(scores - top).astype(BF16)
-        total = jnp.sum(weights.astype(F32), axis=1, keepdims=True)
-        acc = jnp.dot(weights, kv_ref[0, 1, :used, cols], preferred_element_type=F32)
-        for g in range(group):
-            h = k * group + g
-            rows = slice(g * FAN, (g + 1) * FAN)
-            acc_ref[:, h * HEAD_SIZE:(h + 1) * HEAD_SIZE] = acc[rows]
-            tops = jnp.where(lane == h, top[rows], tops)
-            totals = jnp.where(lane == h, total[rows], totals)
-    top_ref[...] = tops
-    total_ref[...] = totals
-
-
-def attend_cache(queries, cache, lengths):
-    prompts, _, slots, width = cache.shape
-    rows, q_width = queries.shape
-    return pl.pallas_call(
-        cache_kernel,
-        out_shape=(
-            jax.ShapeDtypeStruct((rows, q_width), F32),
-            jax.ShapeDtypeStruct((rows, 128), F32),
-            jax.ShapeDtypeStruct((rows, 128), F32),
-        ),
-        grid_spec=pltpu.PrefetchScalarGridSpec(
-            num_scalar_prefetch=1,
-            grid=(prompts,),
-            in_specs=[
-                pl.BlockSpec((FAN, q_width), lambda p, n: (p, 0)),
-                pl.BlockSpec((1, 2, slots, width), lambda p, n: (p, 0, 0, 0)),
-            ],
-            out_specs=(
-                pl.BlockSpec((FAN, q_width), lambda p, n: (p, 0)),
-                pl.BlockSpec((FAN, 128), lambda p, n: (p, 0)),
-                pl.BlockSpec((FAN, 128), lambda p, n: (p, 0)),
-            ),
-        ),
-        compiler_params=pltpu.CompilerParams(vmem_limit_bytes=58 * 2**20),
-        cost_estimate=pl.CostEstimate(
-            flops=4 * rows * q_width * slots, bytes_accessed=2 * cache.size + 4 * rows * q_width,
-            transcendentals=rows * q_width // HEAD_SIZE * slots,
-        ),
-    )(lengths, queries, cache)
+
+    def pair(i, carry):
+        base = pl.multiple_of(i * 2 * FAN, 2 * FAN)
+        loads(i).wait()
+        both = q_ref[pl.ds(base, 2 * FAN), :].astype(F32)
+        for n in range(2):
+            q = both[n * FAN:(n + 1) * FAN]
+            length = length_ref[2 * i + n][:1, :1]
+            tops = jnp.zeros((FAN, 128), F32)
+            totals = jnp.zeros((FAN, 128), F32)
+            out_rows = pl.ds(pl.multiple_of(base + n * FAN, FAN), FAN)
+            for k in range(kv_heads):
+                cols = slice(k * HEAD_SIZE, (k + 1) * HEAD_SIZE)
+                stack = jnp.concatenate(
+                    [q[:, (k * group + g) * HEAD_SIZE:(k * group + g + 1) * HEAD_SIZE] for g in range(group)], axis=0
+                ).astype(BF16)
+                scores = lax.dot_general(
+                    stack, cache[2 * i + n, 0, :, cols], (((1,), (1,)), ((), ())), preferred_element_type=F32
+                ) * SCALE
+                slot = lax.broadcasted_iota(jnp.int32, scores.shape, 1)
+                scores = jnp.where(slot < length, scores, -jnp.inf)
+                top = jnp.max(scores, axis=1, keepdims=True)
+                weights = jnp.exp(scores - top).astype(BF16)
+                total = jnp.sum(weights.astype(F32), axis=1, keepdims=True)
+                acc = jnp.dot(weights, cache[2 * i + n, 1, :, cols], preferred_element_type=F32)
+                for g in range(group):
+                    h = k * group + g
+                    rows = slice(g * FAN, (g + 1) * FAN)
+                    acc_ref[out_rows, h * HEAD_SIZE:(h + 1) * HEAD_SIZE] = acc[rows]
+                    tops = jnp.where(lane == h, top[rows], tops)
+                    totals = jnp.where(lane == h, total[rows], totals)
+            top_ref[out_rows, :] = tops
+            total_ref[out_rows, :] = totals
+        return carry
+
+    lax.fori_loop(0, prompts // 2, pair, 0)
 
 
 W_CHUNKS = 4
@@ -97,11 +66,13 @@
 
 def rows_kernel(
     adapters, tensors, cap,
-    near_ref, far_ref, gain_ref, weight_hbm, down_hbm, up_ref, pick_ref, place_ref, ids_ref,
-    q_ref, acc_ref, top_ref, total_ref,
+    near_ref, gain_ref, weight_hbm, down_hbm, cache_hbm, up_ref, pick_ref, place_ref, ids_ref,
+    q_ref, length_ref,
     new_kv_ref, attn_ref,
-    weight, down, normed, out_rows, in_rows, low_out, low_in, delta, back, base,
-    weight_sem, down_sem, row_send, row_recv, low_send, low_recv, back_send, back_recv,
+    weight, down, cache, acc_ref, top_ref, total_ref, far_ref, square_out, square_in,
+    normed, out_rows, in_rows, low_out, low_in, delta, back, base,
+    weight_sem, down_sem, cache_sem, far_sem, square_sem,
+    row_send, row_recv, low_send, low_recv, back_send, back_recv,
 ):
     a = lax.axis_index("adapter")
     t = lax.axis_index("tensor")
@@ -121,6 +92,14 @@
     load_down = pltpu.make_async_copy(down_hbm, down, down_sem)
     load_down.start()
 
+    def load_cache(i):
+        return pltpu.make_async_copy(
+            cache_hbm.at[pl.ds(2 * i, 2)], cache.at[pl.ds(2 * i, 2)], cache_sem.at[i]
+        )
+
+    for i in range(cache.shape[0] // 2):
+        load_cache(i).start()
+
     barrier = pltpu.get_barrier_semaphore()
 
     def greet_adapter(d, carry):
@@ -133,27 +112,43 @@
 
     core = lax.rem(t, 2)
     square = jnp.zeros((rows, 128), F32)
-    for half_ref in (near_ref, far_ref):
-        for i in range(2):
-            part = half_ref[:, i * quarter:(i + 1) * quarter].astype(F32)
-            part = part * part
-            for j in range(quarter // 128):
-                square = square + part[:, j * 128:(j + 1) * 128]
-    inverse = lax.rsqrt(jnp.sum(square, axis=1, keepdims=True) / width + EPSILON)
-    for half_ref, parity in ((near_ref, core), (far_ref, 1 - core)):
+    for i in range(2):
+        part = near_ref[:, i * quarter:(i + 1) * quarter].astype(F32)
+        part = part * part
+        for j in range(quarter // 128):
+            square = square + part[:, j * 128:(j + 1) * 128]
+    square_out[...] = square
+
+    pl.semaphore_wait(barrier, adapters - 1 + tensors - 1)
+    beside = t + 1 - 2 * core
+    send_square = pltpu.make_async_remote_copy(
+        src_ref=square_out, dst_ref=square_in, send_sem=square_sem.at[0], recv_sem=square_sem.at[1],
+        device_id=(a, beside), device_id_type=MESH,
+    )
+    send_square.start()
+    send_half = pltpu.make_async_remote_copy(
+        src_ref=near_ref, dst_ref=far_ref, send_sem=far_sem.at[0], recv_sem=far_sem.at[1],
+        device_id=(a, beside), device_id_type=MESH,
+    )
+    send_half.start()
+    send_square.wait()
+    both = square + square_in[...]
+    inverse = lax.rsqrt(jnp.sum(both, axis=1, keepdims=True) / width + EPSILON)
+
+    def normalize(half_ref, parity):
         for i in range(2):
             cols = pl.ds(pl.multiple_of((2 * i + parity) * quarter, quarter), quarter)
             normed[:, cols] = (
                 half_ref[:, i * quarter:(i + 1) * quarter].astype(F32) * inverse * gain_ref[:, cols].astype(F32)
             ).astype(BF16)
 
+    normalize(near_ref, core)
     mine = normed[:, pl.ds(pl.multiple_of(t * quarter, quarter), quarter)]
     out_rows[:, :, :quarter] = jnp.dot(
         pick_ref[...], mine, preferred_element_type=F32
     ).astype(BF16).reshape(adapters, cap, quarter)
     out_rows[:, :, quarter:] = ids_ref[...].reshape(adapters, cap, 128)
 
-    pl.semaphore_wait(barrier, adapters - 1 + tensors - 1)
 
     def row_copy(d):
         other = lax.rem(a + d, adapters)
@@ -193,6 +188,9 @@
     each(lambda d: row_copy(d).start())
     in_rows[a] = out_rows[a]
 
+    attend_cache(q_ref, cache, length_ref, load_cache, acc_ref, top_ref, total_ref)
+    send_half.wait()
+    normalize(far_ref, 1 - core)
     for i in range(W_CHUNKS):
         loads[i].wait()
         part = jnp.dot(
@@ -267,7 +265,7 @@
 
 
 def finish_rows(
-    adapters, tensors, cap, near, far, gain, weight, down, up, pick, place, ids, queries, acc, top, total
+    adapters, tensors, cap, near, gain, weight, down, cache, up, pick, place, ids, queries, lengths
 ):
     rows, width = near.shape[0], weight.shape[0]
     columns = weight.shape[1]
@@ -282,11 +280,18 @@
             jax.ShapeDtypeStruct((rows, columns), BF16),
             jax.ShapeDtypeStruct(queries.shape, BF16),
         ),
-        in_specs=[vmem, vmem, vmem, hbm, hbm, vmem, vmem, vmem, vmem, vmem, vmem, vmem, vmem],
+        in_specs=[vmem, vmem, hbm, hbm, hbm, vmem, vmem, vmem, vmem, vmem, vmem],
         out_specs=(vmem, vmem),
         scratch_shapes=[
             pltpu.VMEM(weight.shape, BF16),
             pltpu.VMEM(down.shape, BF16),
+            pltpu.VMEM(cache.shape, BF16),
+            pltpu.VMEM(queries.shape, F32),
+            pltpu.VMEM((rows, 128), F32),
+            pltpu.VMEM((rows, 128), F32),
+            pltpu.VMEM(near.shape, BF16),
+            pltpu.VMEM((rows, 128), F32),
+            pltpu.VMEM((rows, 128), F32),
             pltpu.VMEM((rows, width), BF16),
             pltpu.VMEM((adapters, cap, quarter + 128), BF16),
             pltpu.VMEM((adapters, cap, quarter + 128), BF16),
@@ -297,6 +302,9 @@
             pltpu.VMEM((rows, columns), F32),
             dma((W_CHUNKS,)),
             dma,
+            dma((cache.shape[0] // 2,)),
+            dma((2,)),
+            dma((2,)),
             dma((adapters,)),
             dma((adapters,)),
             dma((tensors,)),
@@ -305,13 +313,13 @@
             dma((adapters,)),
         ],
         compiler_params=pltpu.CompilerParams(
-            collective_id=0, has_side_effects=True, vmem_limit_bytes=59 * 2**20
+            collective_id=0, has_side_effects=True, vmem_limit_bytes=50 * 2**20
         ),
         cost_estimate=pl.CostEstimate(
             flops=2 * rows * width * columns + 2 * slots * down.size, bytes_accessed=2 * (weight.size + down.size),
             transcendentals=0,
         ),
-    )(near, far, gain, weight, down, up, pick, place, ids, queries, acc, top, total)
+    )(near, gain, weight, down, cache, up, pick, place, ids, queries, lengths)
 
 
 def per_device(
@@ -355,24 +363,22 @@
             [lax.dynamic_slice_in_dim(array, (2 * i + parity) * quarter, quarter, 1) for i in range(2)], axis=1
         )
 
+    gain = attention_norm_gain[None, :]
+    lengths = jnp.broadcast_to(prompt_cache_length[:, None, None], (prompt_cache_length.shape[0], 8, 128))
     taken = lax.ppermute(quarters(partials[0], 1 - core), "tensor", swap_core)
+    taken, pick, place, ids, gain, lengths = lax.optimization_barrier((taken, pick, place, ids, gain, lengths))
     chip_sum = (quarters(partials[0], core).astype(F32) + taken.astype(F32)).astype(BF16)
     other_sum = lax.ppermute(chip_sum, "tensor", swap_chip)
     flat_weight = key_value_weight.reshape(width, -1)
     flat_up = adapter_up_weight.reshape(adapter_up_weight.shape[0], -1)
-    acc, top, total = attend_cache(queries, key_value_cache, prompt_cache_length)
-    other_sum, acc, top, total, flat_weight, flat_up, pick, place, ids = lax.optimization_barrier(
-        (other_sum, acc, top, total, flat_weight, flat_up, pick, place, ids)
-    )
+    other_sum, flat_weight, flat_up = lax.optimization_barrier((other_sum, flat_weight, flat_up))
     near = (
         quarters(residual, core).astype(F32) + (chip_sum.astype(F32) + other_sum.astype(F32))
     ).astype(BF16)
-    far = lax.ppermute(near, "tensor", swap_core)
     hidden_part = lax.dynamic_slice_in_dim(near, (t // 2) * quarter, quarter, 1)
-
     new_kv, attended = finish_rows(
-        adapters, tensors, cap, near, far, attention_norm_gain[None, :],
-        flat_weight, adapter_down_weight, flat_up, pick, place, ids, queries, acc, top, total,
+        adapters, tensors, cap, near, gain, flat_weight, adapter_down_weight, key_value_cache, flat_up,
+        pick, place, ids, queries, lengths,
     )
     return hidden_part, new_kv.reshape(rows, key_value_weight.shape[1], 2 * HEAD_SIZE), attended
 

time: 78.9 us -> 68.8 us (0.87)
  Pallas kernels: 54.4 us -> 45.8 us
  waiting for transfers between devices: 0.47 us -> 1.96 us
  local copies, waits for them, and re-layouts: 16.9 us -> 15.5 us
  other arithmetic: 2.65 us -> 1.43 us
    pallas_call x1 -> x0, Pallas kernels: 10.1 us -> none  [attend_cache(): pl.pallas_call(cache_kernel, out_shape=(jax.ShapeDtypeStruct((rows, q_wid...]
    ppermute x1, waiting for transfers between devices: 0.01 us -> 1.96 us  [per_device(): other_sum = lax.ppermute(chip_sum, 'tensor', swap_chip)]
    unnamed x13 -> x5, local copies, waits for them, and re-layouts: 11.9 us -> 10.2 us
    pallas_call x1, Pallas kernels: 44.2 us -> 45.8 us  [finish_rows(): pl.pallas_call(functools.partial(rows_kernel, adapters, tensors, cap), ou...]
    dynamic_slice x2, local copies, waits for them, and re-layouts: 1.34 us -> 2.36 us  [quarters(): lax.dynamic_slice_in_dim(array, (2 * i + parity) * quarter, quarter, 1)]
    reshape x1, local copies, waits for them, and re-layouts: 1.49 us -> 0.65 us  [per_device(): new_kv.reshape(rows, key_value_weight.shape[1], 2 * HEAD_SIZE)]
  transfers between devices with their start and end apart: 3 -> 2, of which waited for: 1 -> 1; matrix products, arithmetic and copies ran while one was open for 17% -> 18% of each run, Pallas kernels for 13% -> 0%
where the time goes in v3:
time: 68.8 us; the launch traced here: 68.6 us
  Pallas kernels  45.8 us (67%)
  local copies, waits for them, and re-layouts  15.5 us (23%)
  starting transfers between devices  3.13 us (5%)
  waiting for transfers between devices  1.96 us (3%)
  other arithmetic  1.43 us (2%)
  between operations  0.76 us (1%)
    pallas_call x1, Pallas kernels, finish_rows(): pl.pallas_call(functools.partial(rows_kernel, adapters, tensors, cap), ou...  45.8 us
    unnamed x5, local copies, waits for them, and re-layouts  10.2 us
    ppermute x1, starting transfers between devices, per_device(): other_sum = lax.ppermute(chip_sum, 'tensor', swap_chip)  2.61 us
    dynamic_slice x2, local copies, waits for them, and re-layouts, quarters(): lax.dynamic_slice_in_dim(array, (2 * i + parity) * quarter, quarter, 1)  2.36 us
    ppermute x1, waiting for transfers between devices, per_device(): other_sum = lax.ppermute(chip_sum, 'tensor', swap_chip)  1.96 us
  transfers between devices with their start and end apart: 2, of which 1 were waited for; matrix products, arithmetic and copies ran while one was open for 18% of the time, Pallas kernels for 0%

profile of v3, /device:TPU:0, one launch (start us, length us, event | category | flops | bytes accessed | tf_op | source)
XLA Modules:
  0.0 68.6 jit_solution(17966549230743580240)
XLA Ops:
  0.7 1.3 %dynamic-slice_bitcast_fusion.3 = (bf16[64,2048]{1,0:T(8,128)(2,1)S(1)}, bf16[64,2048]{1,0:T(8,128)(2,1)S(1)}, bf16[64,2048]{1,0:T(8,128)(2,1)S(1)}, bf16[64,2048]{1,0:T(8,128)(2,1)S(1)}) fusion(bf16[1,64,8192]{2,1,0:T(8,128)(2,1)} %param.10, s32[]{:T(128)S(6)} %select_n.44, s32[]{:T(128)S(6)} %select_n.45, s32[]{:T(128)S(6)} %select_n.47, s32[]{:T(128)S(6)} %select_n.46), kind=kLoop, calls=%fused_computation.6 | loop fusion | bytes 2097168 | tf_op jit(solution)/shard_map/dynamic_slice | solution.py:363
  2.0 0.5 collective-permute-start
  2.5 0.7 fusion.3
  3.2 0.2 convert_reduce_fusion
  3.4 0.1 select_reduce_fusion
  3.5 0.7 %broadcast_in_dim.21.gain_ref = bf16[1,8192]{1,0:T(2,128)(2,1)S(1)} reshape(bf16[8192]{0:T(1024)(128)(2,1)} %param.12) | data formatting | bytes 32768 | tf_op jit(solution)/shard_map/broadcast_in_dim | solution.py:366
  4.3 0.1 fusion.1.place_ref
  4.4 0.0 collective-permute-done
  4.4 0.7 %broadcast_in_dim.22.length_ref = s32[8,8,128]{2,1,0:T(8,128)S(1)} broadcast(s32[8]{0:T(128)} %param.19), dimensions={0} | broadcast | bytes 32800 | tf_op jit(solution)/shard_map/broadcast_in_dim | solution.py:367
  5.1 0.1 broadcast_in_dim.20.ids_ref
  5.2 0.1 add_convert_fusion.1
  5.3 2.6 %collective-permute-start.1 = (bf16[64,4096]{1,0:T(8,128)(2,1)S(1)}, bf16[64,4096]{1,0:T(8,128)(2,1)S(1)}, u32[]{:S(2)}, u32[]{:S(2)}) collective-permute-start(bf16[64,4096]{1,0:T(8,128)(2,1)S(1)} %add_convert_fusion.1), channel_id=1, source_target_pairs={{0,2},{1,3},{2,0},{3,1},{4,6},{5,7},{6,4},{7,5},{8,10},{9,11},{10,... | collective-permute-start | bytes 1572872 | tf_op jit(solution)/shard_map/ppermute | solution.py:371
  8.0 1.4 %copy.14 = bf16[128,8,2,256]{3,1,2,0:T(8,128)(2,1)S(1)} copy(bf16[128,8,2,256]{3,2,1,0:T(2,128)(2,1)} %bitcast.15) | data formatting | bytes 2097152
  9.4 0.0 copy-start
  9.4 8.0 %copy.13 = bf16[1024,8,2,256]{3,1,2,0:T(8,128)(2,1)} copy(bf16[1024,8,2,256]{3,2,1,0:T(2,128)(2,1)} %bitcast.14) | data formatting | bytes 16777216
  17.5 1.1 %constant_dynamic-slice_fusion.2 = (bf16[64,2048]{1,0:T(8,128)(2,1)S(1)}, bf16[64,2048]{1,0:T(8,128)(2,1)S(1)}) fusion(bf16[64,8192]{1,0:T(8,128)(2,1)} %param.11, s32[]{:T(128)S(6)} %select_n.44, s32[]{:T(128)S(6)} %select_n.45), kind=kLoop, calls=%fused_computation.19 | loop fusion | bytes 1048584 | tf_op jit(solution)/shard_map/dynamic_slice | solution.py:363
  18.5 2.0 %collective-permute-done.1 = bf16[64,4096]{1,0:T(8,128)(2,1)S(1)} collective-permute-done((bf16[64,4096]{1,0:T(8,128)(2,1)S(1)}, bf16[64,4096]{1,0:T(8,128)(2,1)S(1)}, u32[]{:S(2)}, u32[]{:S(2)}) %collective-permute-start.1) | collective-permute-done | bytes 524320 | tf_op jit(solution)/shard_map/ppermute | solution.py:371
  20.5 0.2 add_convert_fusion.near_ref
  20.7 0.7 %constant_dynamic-slice_fusion = bf16[64,2048]{1,0:T(8,128)(2,1)} fusion(bf16[64,4096]{1,0:T(8,128)(2,1)S(1)} %add_convert_fusion.near_ref, s32[]{:T(128)S(6)} %select_n.52), kind=kLoop, calls=%fused_computation.17 | loop fusion | bytes 524292 | tf_op jit(solution)/shard_map/dynamic_slice | solution.py:378
  21.4 0.0 copy-done
  21.4 45.8 %shard_map.121 = (bf16[64,512]{1,0:T(8,128)(2,1)S(1)}, bf16[64,2048]{1,0:T(8,128)(2,1)S(1)}) custom-call(bf16[64,4096]{1,0:T(8,128)(2,1)S(1)} %add_convert_fusion.near_ref, bf16[1,8192]{1,0:T(2,128)(2,1)S(1)} %broadcast_in_dim.21.gain_ref, bf16[8192,512]{1,0:T(8,128)(2,1)} %bitcast.13, bf16[2048,1024]{1,0:T(8,128)(2,1)} %down_hbm.1, ...), custom_call_target="tpu_custom_call" | custom-call | flops 1610612736 | bytes 12582912 | tf_op jit(solution)/shard_map/pallas_call | solution.py:277
  67.2 0.6 reshape.31
  67.9 0.7 %copy.16 = bf16[64,2048]{1,0:T(8,128)(2,1)} copy(bf16[64,2048]{1,0:T(8,128)(2,1)S(1)} %get-tuple-element.38) | data formatting | bytes 524288
  (4 shorter events, 0.1 us)
Async XLA Ops:
  2.0 2.4 %collective-permute-start = (bf16[64,4096]{1,0:T(8,128)(2,1)S(1)}, bf16[64,4096]{1,0:T(8,128)(2,1)S(1)}, u32[]{:S(2)}, u32[]{:S(2)}) collective-permute-start(bf16[64,4096]{1,0:T(8,128)(2,1)S(1)} %pad_maximum_fusion), channel_id=1, source_target_pairs={{0,1},{1,0},{2,3},{3,2},{4,5},{5,4},{6,7},{7,6},{8,9},{9,8},{10,11... | collective-permute-start | bytes 1572872 | tf_op jit(solution)/shard_map/ppermute | solution.py:368
  5.3 15.2 %collective-permute-start.1 = (bf16[64,4096]{1,0:T(8,128)(2,1)S(1)}, bf16[64,4096]{1,0:T(8,128)(2,1)S(1)}, u32[]{:S(2)}, u32[]{:S(2)}) collective-permute-start(bf16[64,4096]{1,0:T(8,128)(2,1)S(1)} %add_convert_fusion.1), channel_id=1, source_target_pairs={{0,2},{1,3},{2,0},{3,1},{4,6},{5,7},{6,4},{7,5},{8,10},{9,11},{10,... | collective-permute-start | bytes 1572872 | tf_op jit(solution)/shard_map/ppermute | solution.py:371
  9.4 12.0 %copy-start = (bf16[64,2048]{1,0:T(8,128)(2,1)S(1)}, bf16[64,2048]{1,0:T(8,128)(2,1)}, u32[]{:S(2)}) copy-start(bf16[64,2048]{1,0:T(8,128)(2,1)} %q_ref.1) | copy-start | bytes 786436

commit v4 on v3

--- a/solution.py
+++ b/solution.py
@@ -70,7 +70,7 @@
     q_ref, length_ref,
     new_kv_ref, attn_ref,
     weight, down, cache, acc_ref, top_ref, total_ref, far_ref, square_out, square_in,
-    normed, out_rows, in_rows, low_out, low_in, delta, back, base,
+    normed, out_rows, in_rows, low_own, low_out, low_in, delta, back, base,
     weight_sem, down_sem, cache_sem, far_sem, square_sem,
     row_send, row_recv, low_send, low_recv, back_send, back_recv,
 ):
@@ -199,18 +199,35 @@
         base[...] = part if i == 0 else base[...] + part
     load_down.wait()
 
-    each(lambda d: row_arrival(d).wait_recv())
-
-    lane = lax.broadcasted_iota(jnp.int32, (slots, 128), 1)
-    odd = jnp.where(lane >= ADAPTER_RANK, 1.0, 0.0)
+    side = adapters // 2
+    for far in range(2):
+        first = lax.rem(a // side + far, 2) * side
+
+        def arrive(i, carry):
+            d = lax.rem(first + i - a + adapters, adapters)
+
+            @pl.when(d > 0)
+            def _():
+                row_arrival(d).wait_recv()
+
+            return carry
+
+        lax.fori_loop(0, side, arrive, 0)
+        some = slots // 2
+        odd = jnp.where(lax.broadcasted_iota(jnp.int32, (some, 128), 1) >= ADAPTER_RANK, 1.0, 0.0)
+        block = in_rows[pl.ds(first, side)]
+        ids = block[:, :, quarter:].reshape(some, 128).astype(F32) - odd
+        got = block[:, :, :quarter].reshape(some, quarter)
+        low = jnp.zeros((some, 128), F32)
+        wide = 2
+        for j in range(0, down.shape[1] // 128, wide):
+            part = jnp.dot(got, down[:, j * 128:(j + wide) * 128], preferred_element_type=F32)
+            for i in range(wide):
+                low = low + jnp.where(ids == 2.0 * (j + i), part[:, i * 128:(i + 1) * 128], 0.0)
+        low_own[pl.ds(pl.multiple_of(first * cap, some), some), :] = low
+    low = low_own[...]
+    odd = jnp.where(lax.broadcasted_iota(jnp.int32, (slots, 128), 1) >= ADAPTER_RANK, 1.0, 0.0)
     ids = in_rows[:, :, quarter:].reshape(slots, 128).astype(F32) - odd
-    got = in_rows[:, :, :quarter].reshape(slots, quarter)
-    low = jnp.zeros((slots, 128), F32)
-    wide = 2
-    for j in range(0, down.shape[1] // 128, wide):
-        part = jnp.dot(got, down[:, j * 128:(j + wide) * 128], preferred_element_type=F32)
-        for i in range(wide):
-            low = low + jnp.where(ids == 2.0 * (j + i), part[:, i * 128:(i + 1) * 128], 0.0)
     low_out[...] = low.astype(BF16)
 
     shares = []
@@ -295,6 +312,7 @@
             pltpu.VMEM((rows, width), BF16),
             pltpu.VMEM((adapters, cap, quarter + 128), BF16),
             pltpu.VMEM((adapters, cap, quarter + 128), BF16),
+            pltpu.VMEM((slots, 128), F32),
             pltpu.VMEM((slots, 128), BF16),
             pltpu.VMEM((tensors, slots, 128), BF16),
             pltpu.VMEM((adapters, cap, columns), BF16),

time: 68.8 us -> 68.4 us (level)
  no operation moved by 1% of the time
where the time goes in v4:
time: 68.4 us; the launch traced here: 68.1 us
  Pallas kernels  45.3 us (66%)
  local copies, waits for them, and re-layouts  15.5 us (23%)
  starting transfers between devices  3.13 us (5%)
  waiting for transfers between devices  1.96 us (3%)
  other arithmetic  1.43 us (2%)
  between operations  0.76 us (1%)
    pallas_call x1, Pallas kernels, finish_rows(): pl.pallas_call(functools.partial(rows_kernel, adapters, tensors, cap), ou...  45.3 us
    unnamed x5, local copies, waits for them, and re-layouts  10.2 us
    ppermute x1, starting transfers between devices, per_device(): other_sum = lax.ppermute(chip_sum, 'tensor', swap_chip)  2.61 us
    dynamic_slice x2, local copies, waits for them, and re-layouts, quarters(): lax.dynamic_slice_in_dim(array, (2 * i + parity) * quarter, quarter, 1)  2.36 us
    ppermute x1, waiting for transfers between devices, per_device(): other_sum = lax.ppermute(chip_sum, 'tensor', swap_chip)  1.96 us
  transfers between devices with their start and end apart: 2, of which 1 were waited for; matrix products, arithmetic and copies ran while one was open for 18% of the time, Pallas kernels for 0%

profile of v4, /device:TPU:0, one launch (start us, length us, event | category | flops | bytes accessed | tf_op | source)
XLA Modules:
  0.0 68.1 jit_solution(1992028304220540893)
XLA Ops:
  0.7 1.3 %dynamic-slice_bitcast_fusion.3 = (bf16[64,2048]{1,0:T(8,128)(2,1)S(1)}, bf16[64,2048]{1,0:T(8,128)(2,1)S(1)}, bf16[64,2048]{1,0:T(8,128)(2,1)S(1)}, bf16[64,2048]{1,0:T(8,128)(2,1)S(1)}) fusion(bf16[1,64,8192]{2,1,0:T(8,128)(2,1)} %param.10, s32[]{:T(128)S(6)} %select_n.44, s32[]{:T(128)S(6)} %select_n.45, s32[]{:T(128)S(6)} %select_n.47, s32[]{:T(128)S(6)} %select_n.46), kind=kLoop, calls=%fused_computation.6 | loop fusion | bytes 2097168 | tf_op jit(solution)/shard_map/dynamic_slice | solution.py:381
  2.0 0.5 collective-permute-start
  2.5 0.7 fusion.3
  3.2 0.2 convert_reduce_fusion
  3.4 0.1 select_reduce_fusion
  3.5 0.7 %broadcast_in_dim.21.gain_ref = bf16[1,8192]{1,0:T(2,128)(2,1)S(1)} reshape(bf16[8192]{0:T(1024)(128)(2,1)} %param.12) | data formatting | bytes 32768 | tf_op jit(solution)/shard_map/broadcast_in_dim | solution.py:384
  4.3 0.1 fusion.1.place_ref
  4.4 0.0 collective-permute-done
  4.4 0.7 %broadcast_in_dim.22.length_ref = s32[8,8,128]{2,1,0:T(8,128)S(1)} broadcast(s32[8]{0:T(128)} %param.19), dimensions={0} | broadcast | bytes 32800 | tf_op jit(solution)/shard_map/broadcast_in_dim | solution.py:385
  5.1 0.1 broadcast_in_dim.20.ids_ref
  5.2 0.1 add_convert_fusion.1
  5.3 2.6 %collective-permute-start.1 = (bf16[64,4096]{1,0:T(8,128)(2,1)S(1)}, bf16[64,4096]{1,0:T(8,128)(2,1)S(1)}, u32[]{:S(2)}, u32[]{:S(2)}) collective-permute-start(bf16[64,4096]{1,0:T(8,128)(2,1)S(1)} %add_convert_fusion.1), channel_id=1, source_target_pairs={{0,2},{1,3},{2,0},{3,1},{4,6},{5,7},{6,4},{7,5},{8,10},{9,11},{10,... | collective-permute-start | bytes 1572872 | tf_op jit(solution)/shard_map/ppermute | solution.py:389
  8.0 1.4 %copy.14 = bf16[128,8,2,256]{3,1,2,0:T(8,128)(2,1)S(1)} copy(bf16[128,8,2,256]{3,2,1,0:T(2,128)(2,1)} %bitcast.15) | data formatting | bytes 2097152
  9.4 0.0 copy-start
  9.4 8.0 %copy.13 = bf16[1024,8,2,256]{3,1,2,0:T(8,128)(2,1)} copy(bf16[1024,8,2,256]{3,2,1,0:T(2,128)(2,1)} %bitcast.14) | data formatting | bytes 16777216
  17.5 1.1 %constant_dynamic-slice_fusion.2 = (bf16[64,2048]{1,0:T(8,128)(2,1)S(1)}, bf16[64,2048]{1,0:T(8,128)(2,1)S(1)}) fusion(bf16[64,8192]{1,0:T(8,128)(2,1)} %param.11, s32[]{:T(128)S(6)} %select_n.44, s32[]{:T(128)S(6)} %select_n.45), kind=kLoop, calls=%fused_computation.19 | loop fusion | bytes 1048584 | tf_op jit(solution)/shard_map/dynamic_slice | solution.py:381
  18.5 2.0 %collective-permute-done.1 = bf16[64,4096]{1,0:T(8,128)(2,1)S(1)} collective-permute-done((bf16[64,4096]{1,0:T(8,128)(2,1)S(1)}, bf16[64,4096]{1,0:T(8,128)(2,1)S(1)}, u32[]{:S(2)}, u32[]{:S(2)}) %collective-permute-start.1) | collective-permute-done | bytes 524320 | tf_op jit(solution)/shard_map/ppermute | solution.py:389
  20.5 0.2 add_convert_fusion.near_ref
  20.7 0.7 %constant_dynamic-slice_fusion = bf16[64,2048]{1,0:T(8,128)(2,1)} fusion(bf16[64,4096]{1,0:T(8,128)(2,1)S(1)} %add_convert_fusion.near_ref, s32[]{:T(128)S(6)} %select_n.52), kind=kLoop, calls=%fused_computation.17 | loop fusion | bytes 524292 | tf_op jit(solution)/shard_map/dynamic_slice | solution.py:396
  21.4 0.0 copy-done
  21.4 45.3 %shard_map.121 = (bf16[64,512]{1,0:T(8,128)(2,1)S(1)}, bf16[64,2048]{1,0:T(8,128)(2,1)S(1)}) custom-call(bf16[64,4096]{1,0:T(8,128)(2,1)S(1)} %add_convert_fusion.near_ref, bf16[1,8192]{1,0:T(2,128)(2,1)S(1)} %broadcast_in_dim.21.gain_ref, bf16[8192,512]{1,0:T(8,128)(2,1)} %bitcast.13, bf16[2048,1024]{1,0:T(8,128)(2,1)} %down_hbm.1, ...), custom_call_target="tpu_custom_call" | custom-call | flops 1610612736 | bytes 12582912 | tf_op jit(solution)/shard_map/pallas_call | solution.py:294
  66.8 0.6 reshape.31
  67.4 0.7 %copy.16 = bf16[64,2048]{1,0:T(8,128)(2,1)} copy(bf16[64,2048]{1,0:T(8,128)(2,1)S(1)} %get-tuple-element.38) | data formatting | bytes 524288
  (4 shorter events, 0.1 us)
Async XLA Ops:
  2.0 2.4 %collective-permute-start = (bf16[64,4096]{1,0:T(8,128)(2,1)S(1)}, bf16[64,4096]{1,0:T(8,128)(2,1)S(1)}, u32[]{:S(2)}, u32[]{:S(2)}) collective-permute-start(bf16[64,4096]{1,0:T(8,128)(2,1)S(1)} %pad_maximum_fusion), channel_id=1, source_target_pairs={{0,1},{1,0},{2,3},{3,2},{4,5},{5,4},{6,7},{7,6},{8,9},{9,8},{10,11... | collective-permute-start | bytes 1572872 | tf_op jit(solution)/shard_map/ppermute | solution.py:386
  5.3 15.2 %collective-permute-start.1 = (bf16[64,4096]{1,0:T(8,128)(2,1)S(1)}, bf16[64,4096]{1,0:T(8,128)(2,1)S(1)}, u32[]{:S(2)}, u32[]{:S(2)}) collective-permute-start(bf16[64,4096]{1,0:T(8,128)(2,1)S(1)} %add_convert_fusion.1), channel_id=1, source_target_pairs={{0,2},{1,3},{2,0},{3,1},{4,6},{5,7},{6,4},{7,5},{8,10},{9,11},{10,... | collective-permute-start | bytes 1572872 | tf_op jit(solution)/shard_map/ppermute | solution.py:389
  9.4 12.0 %copy-start = (bf16[64,2048]{1,0:T(8,128)(2,1)S(1)}, bf16[64,2048]{1,0:T(8,128)(2,1)}, u32[]{:S(2)}) copy-start(bf16[64,2048]{1,0:T(8,128)(2,1)} %q_ref.1) | copy-start | bytes 786436
